TPU v7x, 32 devices: a whole 2x2x4 slice. The times are simulated.
32 devices in a mesh: batch: 4 (over y, x), seq: 8 (over z, core).
Axes of the slice: x: 2, y: 2, z: 4, core: 2. Of those that a mesh axis runs over, the one named last changes fastest.
Arguments:
- hidden_in: bfloat16 [8, 1024, 2048], P('batch', 'seq'), may hold values from -6 to 6
- lengths: int32 [8], replicated, may hold values from 256 to 1024, as said below
- q_weight: bfloat16 [2048, 256], P(('batch', 'seq')), may hold values from -0.125 to 0.125
- k_weight: bfloat16 [2048, 256], P(('batch', 'seq')), may hold values from -0.125 to 0.125
- v_weight: bfloat16 [2048, 2048], P(('batch', 'seq')), may hold values from -0.125 to 0.125
- out_weight: bfloat16 [2048, 2048], P(None, ('batch', 'seq')), may hold values from -2 to 2
- conv_weight: bfloat16 [2048, 3], P(('batch', 'seq')), may hold values from -3 to 3
- norm_attn: bfloat16 [2048], P(('batch', 'seq')), may hold values from 0.099609375 to 1.8984375
- gate_weight: bfloat16 [2048, 5504], P(('batch', 'seq')), may hold values from -0.125 to 0.125
- up_weight: bfloat16 [2048, 5504], P(('batch', 'seq')), may hold values from -0.125 to 0.125
- down_weight: bfloat16 [5504, 2048], P(None, ('batch', 'seq')), may hold values from -0.078125 to 0.078125
- norm_mlp: bfloat16 [2048], P(('batch', 'seq')), may hold values from 0.099609375 to 1.8984375
- cotangent: bfloat16 [8, 1024, 2048], P('batch', 'seq'), may hold values from -6 to 6
Outputs:
- hidden_out: bfloat16 [8, 1024, 2048], P('batch', 'seq')
- hidden_grad: float32 [8, 1024, 2048], P('batch', 'seq')
- grad_q: float32 [2048, 256], P(('batch', 'seq'))
- grad_k: float32 [2048, 256], P(('batch', 'seq'))
- grad_v: float32 [2048, 2048], P(('batch', 'seq'))
- grad_out: float32 [2048, 2048], P(None, ('batch', 'seq'))
- grad_conv: float32 [2048, 3], P(('batch', 'seq'))
- grad_norm_attn: float32 [2048], P(('batch', 'seq'))
- grad_gate: float32 [2048, 5504], P(('batch', 'seq'))
- grad_up: float32 [2048, 5504], P(('batch', 'seq'))
- grad_down: float32 [5504, 2048], P(None, ('batch', 'seq'))
- grad_norm_mlp: float32 [2048], P(('batch', 'seq'))
- den_mean: float32 [], replicated
Inputs may be any that keep to these rules, and one draw needn't show every extreme that they name: `lengths`: valid tokens of each sequence counted from its start; later positions are padding. Among the sequences of each index of batch one has 1024 valid tokens.
All inputs are finite; a program needn't handle non-finite values.
Results may differ from a plain program's by a relative error of at most 0.017.
Values may be sent and summed in bfloat16 or wider, within the bound.
No kernel may reach another device: no remote copies, remote signals or barrier semaphores. Data moves between devices by JAX's collectives and lax.ppermute only.
A program may use at most 512 MiB of HBM per device.

v0:
```python
import math

import jax
import jax.numpy as jnp
from jax import lax
from jax.sharding import PartitionSpec as P

HEADS = 16
FEAT = 16
KERNEL = 3


epsilon = 1e-06
highest = lax.Precision.HIGHEST


def from_behind(value, axis, steps):
    count = lax.axis_size(axis)
    initial, last = (max(0, -steps), min(count, count - steps))
    return lax.ppermute(value, axis, [(source, source + steps) for source in range(initial, last)])


def carried_in(part, axis, combine, identity):
    place = lax.axis_index(axis)
    gathered = jax.tree.map(lambda a: lax.all_gather(a, axis), part)
    state = jax.tree.map(lambda a, e: jnp.zeros_like(a) + jnp.asarray(e, a.dtype), part, identity)

    def one(turn, state):
        return combine(
            state, jax.tree.map(lambda a: lax.dynamic_index_in_dim(a, turn, 0, False), gathered)
        )

    return lax.fori_loop(0, place, one, state)


def entering(value, axis, combine, identity):
    count, place = (lax.axis_size(axis), lax.axis_index(axis))
    everything = jax.tree.map(
        lambda part, kind: lax.all_gather(part.astype(kind), axis),
        value,
        (jnp.bfloat16, jnp.bfloat16),
    )
    start = jax.tree.map(
        lambda part, zero: jnp.broadcast_to(jnp.asarray(zero, part.dtype), part.shape),
        value,
        identity,
    )

    def turn(k, before):
        at = count - 1 - k
        reached = at > place
        new = combine(
            before, jax.tree.map(lambda part, own: part[at].astype(own.dtype), everything, value)
        )
        return jax.tree.map(lambda a, b: jnp.where(reached, a, b), new, before)

    return lax.fori_loop(0, count, turn, start)


def rms_norm(v, gain):
    return v * lax.rsqrt(jnp.mean(v * v, axis=-1, keepdims=True) + epsilon) * gain


def features(u):
    feat_width = u.shape[-1]
    quad_terms = (u[..., :, None] * u[..., None, :]).reshape(
        u.shape[:-1] + (feat_width * feat_width,)
    )
    ones_col = jnp.ones(u.shape[:-1] + (1,), u.dtype)
    return jnp.concatenate(
        [ones_col, u * feat_width ** (-0.25), quad_terms / math.sqrt(2.0 * feat_width)], axis=-1
    )


def product(left, right):
    return jnp.dot(left, right, preferred_element_type=jnp.float32)


def outer_sum(left, right):
    return lax.dot_general(
        left, right, (((0,), (0,)), ((), ())), preferred_element_type=jnp.float32
    )


def back_product(left, right):
    return lax.dot_general(
        left, right, (((1,), (1,)), ((), ())), preferred_element_type=jnp.float32
    )


def add_pair(earlier, later):
    return (earlier[0] + later[0], earlier[1] + later[1])


def swiglu_parts(gate_act, up_act):
    sigma_gate = jax.nn.sigmoid(gate_act)
    hidden_act = (gate_act * sigma_gate * up_act).astype(jnp.bfloat16)
    return (sigma_gate, hidden_act)


def swiglu_back(d_hid, gate_act, up_act, sigma_gate):
    d_gate = (d_hid * up_act * sigma_gate * (1.0 + gate_act * (1.0 - sigma_gate))).astype(
        jnp.bfloat16
    )
    d_up = (d_hid * gate_act * sigma_gate).astype(jnp.bfloat16)
    return (d_gate, d_up)


def on_device(
    hidden_in,
    lengths,
    q_weight,
    k_weight,
    v_weight,
    out_weight,
    conv_weight,
    norm_attn,
    gate_weight,
    up_weight,
    down_weight,
    norm_mlp,
    cotangent,
):
    row_count, local_len, model_width = hidden_in.shape
    tokens = row_count * local_len
    head_count = HEADS
    feat_dim = FEAT
    value_dim = model_width // head_count
    lag_width = KERNEL - 1
    seq_place = lax.axis_index("seq")
    seq_len = local_len * lax.axis_size("seq")
    offset = seq_place * local_len
    own_lengths = lax.dynamic_slice_in_dim(
        lengths, lax.axis_index("batch") * row_count, row_count, 0
    )
    total_valid = jnp.sum(lengths).astype(jnp.float32)
    pad_mask = (
        offset + jnp.arange(local_len, dtype=jnp.int32)[None, :] < own_lengths[:, None]
    ).astype(jnp.float32)
    w_query, w_key, w_value, w_out, w_conv, gain_raw, gain_mraw = (
        lax.all_gather(q_weight, ("batch", "seq"), axis=0, tiled=True),
        lax.all_gather(k_weight, ("batch", "seq"), axis=0, tiled=True),
        lax.all_gather(v_weight, ("batch", "seq"), axis=0, tiled=True),
        lax.all_gather(out_weight, ("batch", "seq"), axis=1, tiled=True),
        lax.all_gather(conv_weight, ("batch", "seq"), axis=0, tiled=True),
        lax.all_gather(norm_attn, ("batch", "seq"), axis=0, tiled=True),
        lax.all_gather(norm_mlp, ("batch", "seq"), axis=0, tiled=True),
    )
    gain_attn = gain_raw.astype(jnp.float32)
    gain_mlp = gain_mraw.astype(jnp.float32)
    conv_taps = w_conv.astype(jnp.float32)
    inputs = hidden_in.astype(jnp.float32)
    normed_attn = rms_norm(inputs, gain_attn)
    prev_edge = from_behind(
        normed_attn[:, local_len - lag_width :, :].astype(jnp.bfloat16), "seq", 1
    ).astype(jnp.float32)
    extended = jnp.concatenate([prev_edge, normed_attn], axis=1)
    mixed_in = jnp.zeros_like(normed_attn)
    for j in range(KERNEL):
        mixed_in = (
            mixed_in + conv_taps[:, j] * extended[:, lag_width - j : lag_width - j + local_len, :]
        )
    c_low = mixed_in.astype(jnp.bfloat16).reshape(tokens, model_width)
    queries = product(c_low, w_query)
    keys_raw = product(c_low, w_key)
    values = product(c_low, w_value)
    queries_heads = queries.reshape(row_count, local_len, head_count, feat_dim)
    keys_heads = keys_raw.reshape(row_count, local_len, head_count, feat_dim)
    feat_q = features(queries_heads).astype(jnp.bfloat16)
    feat_k = (features(keys_heads) * pad_mask[:, :, None, None]).astype(jnp.bfloat16)
    v_low = values.astype(jnp.bfloat16).reshape(row_count, local_len, head_count, value_dim)
    local_state = jnp.einsum("rshp,rshv->rhpv", feat_k, v_low, preferred_element_type=jnp.float32)
    feat_k32 = feat_k.astype(jnp.float32)
    local_total = jnp.sum(feat_k32, axis=1)
    zero_pair = (jnp.zeros_like(local_state), jnp.zeros_like(local_total))
    prev_state, prev_total = carried_in((local_state, local_total), "seq", add_pair, zero_pair)
    causal = jnp.tril(jnp.ones((local_len, local_len), jnp.float32))
    feat_q32 = feat_q.astype(jnp.float32)
    value_f32 = v_low.astype(jnp.float32)
    scores = (
        jnp.einsum("rthp,rshp->rhts", feat_q, feat_k, preferred_element_type=jnp.float32) * causal
    )
    numerator = jnp.einsum("rhts,rshv->rthv", scores, value_f32, precision=highest) + jnp.einsum(
        "rthp,rhpv->rthv", feat_q32, prev_state, precision=highest
    )
    denominator = jnp.sum(scores, axis=-1).transpose(0, 2, 1) + jnp.einsum(
        "rthp,rhp->rth", feat_q32, prev_total, precision=highest
    )
    attn_val = numerator / denominator[..., None]
    y_low = attn_val.reshape(tokens, model_width).astype(jnp.bfloat16)
    resid_mid = inputs.reshape(tokens, model_width) + product(y_low, w_out)
    den_total = lax.psum(jnp.sum(denominator * pad_mask[:, :, None]), ("batch", "seq"))
    den_mean = den_total / (head_count * seq_len * total_valid)
    n2_low = rms_norm(resid_mid, gain_mlp).astype(jnp.bfloat16)
    cot_full = cotangent.astype(jnp.float32).reshape(tokens, model_width)
    g_low = cotangent.reshape(tokens, model_width)
    down_local = down_weight.T
    gate_part, up_part, down_part = (
        lax.all_to_all(gate_weight, "seq", split_axis=1, concat_axis=0, tiled=True),
        lax.all_to_all(up_weight, "seq", split_axis=1, concat_axis=0, tiled=True),
        lax.all_to_all(down_local, "seq", split_axis=1, concat_axis=0, tiled=True),
    )
    gate_cols, up_cols, down_cols = (
        lax.all_gather(gate_part, "batch", axis=0, tiled=True),
        lax.all_gather(up_part, "batch", axis=0, tiled=True),
        lax.all_gather(down_part, "batch", axis=0, tiled=True),
    )
    n2_pos = n2_low.reshape(row_count, local_len, model_width).transpose(1, 0, 2)
    cot_pos = g_low.reshape(row_count, local_len, model_width).transpose(1, 0, 2)
    all_n2, all_cot = (
        lax.all_gather(n2_pos, "seq", axis=0, tiled=True),
        lax.all_gather(cot_pos, "seq", axis=0, tiled=True),
    )
    flat_n2 = all_n2.reshape(seq_len * row_count, model_width)
    flat_cot = all_cot.reshape(seq_len * row_count, model_width)
    gate_act = product(flat_n2, gate_cols)
    up_act = product(flat_n2, up_cols)
    sigma_gate, hidden_act = swiglu_parts(gate_act, up_act)
    down_sum = lax.psum_scatter(
        back_product(hidden_act, down_cols)
        .reshape(lax.axis_size("seq") * local_len, row_count, model_width)
        .astype(jnp.bfloat16),
        "seq",
        scatter_dimension=0,
        tiled=True,
    ).astype(jnp.float32)
    block_out = resid_mid + down_sum.transpose(1, 0, 2).reshape(tokens, model_width)
    hidden_out = block_out.astype(jnp.bfloat16).reshape(row_count, local_len, model_width)
    grad_down_part = outer_sum(hidden_act, flat_cot)
    d_hid = product(flat_cot, down_cols)
    d_gate, d_up = swiglu_back(d_hid, gate_act, up_act, sigma_gate)
    grad_gate_part = outer_sum(flat_n2, d_gate)
    grad_up_part = outer_sum(flat_n2, d_up)
    summed = back_product(d_gate, gate_cols) + back_product(d_up, up_cols)
    back_sum = lax.psum_scatter(
        summed.reshape(lax.axis_size("seq") * local_len, row_count, model_width).astype(
            jnp.bfloat16
        ),
        "seq",
        scatter_dimension=0,
        tiled=True,
    ).astype(jnp.float32)
    d_n2 = back_sum.transpose(1, 0, 2).reshape(tokens, model_width)
    gate_rows_sum, up_rows_sum, down_rows_sum = (
        lax.psum_scatter(
            grad_gate_part.astype(jnp.bfloat16), "batch", scatter_dimension=0, tiled=True
        ).astype(jnp.float32),
        lax.psum_scatter(
            grad_up_part.astype(jnp.bfloat16), "batch", scatter_dimension=0, tiled=True
        ).astype(jnp.float32),
        lax.psum_scatter(
            grad_down_part.T.astype(jnp.bfloat16), "batch", scatter_dimension=0, tiled=True
        ).astype(jnp.float32),
    )
    grad_gate, grad_up, down_owned = (
        lax.all_to_all(
            gate_rows_sum.astype(jnp.bfloat16), "seq", split_axis=0, concat_axis=1, tiled=True
        ).astype(gate_rows_sum.dtype),
        lax.all_to_all(
            up_rows_sum.astype(jnp.bfloat16), "seq", split_axis=0, concat_axis=1, tiled=True
        ).astype(up_rows_sum.dtype),
        lax.all_to_all(
            down_rows_sum.astype(jnp.bfloat16), "seq", split_axis=0, concat_axis=1, tiled=True
        ).astype(down_rows_sum.dtype),
    )
    grad_down = down_owned.T
    _, norm_pull = jax.vjp(rms_norm, resid_mid, gain_mlp)
    d_mid_norm, grad_gain_mlp = norm_pull(d_n2)
    d_mid = cot_full + d_mid_norm
    d_attn = d_mid.astype(jnp.bfloat16)
    grad_out_full = outer_sum(y_low, d_attn)
    d_y = back_product(d_attn, w_out).reshape(row_count, local_len, head_count, value_dim)
    d_num = d_y / denominator[..., None]
    d_den = -jnp.sum(d_y * attn_val, axis=-1) / denominator
    back_state = jnp.einsum("rthp,rthv->rhpv", feat_q32, d_num, precision=highest)
    back_total = jnp.einsum("rthp,rth->rhp", feat_q32, d_den, precision=highest)
    later_state, later_total = entering((back_state, back_total), "seq", add_pair, zero_pair)
    weights_ts = (
        jnp.einsum("rthv,rshv->rhts", d_num, value_f32, precision=highest)
        + d_den.transpose(0, 2, 1)[..., None]
    ) * causal
    d_fq = (
        jnp.einsum("rhts,rshp->rthp", weights_ts, feat_k32, precision=highest)
        + jnp.einsum("rhpv,rthv->rthp", prev_state, d_num, precision=highest)
        + prev_total[:, None, :, :] * d_den[..., None]
    )
    d_fk = (
        jnp.einsum("rhts,rthp->rshp", weights_ts, feat_q32, precision=highest)
        + jnp.einsum("rhpv,rshv->rshp", later_state, value_f32, precision=highest)
        + later_total[:, None, :, :]
    )
    d_v = jnp.einsum("rhts,rthv->rshv", scores, d_num, precision=highest) + jnp.einsum(
        "rhpv,rshp->rshv", later_state, feat_k32, precision=highest
    )
    _, query_pull = jax.vjp(features, queries_heads)
    d_q = query_pull(d_fq)[0].reshape(tokens, head_count * feat_dim).astype(jnp.bfloat16)
    _, key_pull = jax.vjp(features, keys_heads)
    d_k = (
        key_pull(d_fk * pad_mask[:, :, None, None])[0]
        .reshape(tokens, head_count * feat_dim)
        .astype(jnp.bfloat16)
    )
    d_v_low = d_v.reshape(tokens, model_width).astype(jnp.bfloat16)
    grad_q_full = outer_sum(c_low, d_q)
    grad_k_full = outer_sum(c_low, d_k)
    grad_v_full = outer_sum(c_low, d_v_low)
    d_c = (
        back_product(d_q, w_query) + back_product(d_k, w_key) + back_product(d_v_low, w_value)
    ).reshape(row_count, local_len, model_width)
    next_edge = from_behind(d_c[:, :lag_width, :].astype(jnp.bfloat16), "seq", -1).astype(
        jnp.float32
    )
    d_extended = jnp.concatenate([d_c, next_edge], axis=1)
    d_n1 = jnp.zeros_like(d_c)
    conv_columns = []
    for j in range(KERNEL):
        d_n1 = d_n1 + conv_taps[:, j] * d_extended[:, j : j + local_len, :]
        conv_columns.append(
            jnp.sum(d_c * extended[:, lag_width - j : lag_width - j + local_len, :], axis=(0, 1))
        )
    grad_conv_full = jnp.stack(conv_columns, axis=1)
    _, first_pull = jax.vjp(rms_norm, inputs, gain_attn)
    d_inputs, grad_gain_attn = first_pull(d_n1)
    hidden_grad = d_mid.reshape(row_count, local_len, model_width) + d_inputs
    grad_q, grad_k, grad_v, grad_out, grad_conv, grad_norm_attn, grad_norm_mlp = (
        lax.psum_scatter(grad_q_full, ("batch", "seq"), scatter_dimension=0, tiled=True),
        lax.psum_scatter(grad_k_full, ("batch", "seq"), scatter_dimension=0, tiled=True),
        lax.psum_scatter(grad_v_full, ("batch", "seq"), scatter_dimension=0, tiled=True),
        lax.psum_scatter(grad_out_full, ("batch", "seq"), scatter_dimension=1, tiled=True),
        lax.psum_scatter(grad_conv_full, ("batch", "seq"), scatter_dimension=0, tiled=True),
        lax.psum_scatter(grad_gain_attn, ("batch", "seq"), scatter_dimension=0, tiled=True),
        lax.psum_scatter(grad_gain_mlp, ("batch", "seq"), scatter_dimension=0, tiled=True),
    )
    return (
        hidden_out,
        hidden_grad,
        grad_q,
        grad_k,
        grad_v,
        grad_out,
        grad_conv,
        grad_norm_attn,
        grad_gate,
        grad_up,
        grad_down,
        grad_norm_mlp,
        den_mean,
    )


def solution(mesh):
    placed = (
        P("batch", "seq", None),
        P(),
        P(("batch", "seq"), None),
        P(("batch", "seq"), None),
        P(("batch", "seq"), None),
        P(None, ("batch", "seq")),
        P(("batch", "seq"), None),
        P(("batch", "seq")),
        P(("batch", "seq"), None),
        P(("batch", "seq"), None),
        P(None, ("batch", "seq")),
        P(("batch", "seq")),
        P("batch", "seq", None),
    )
    return jax.shard_map(
        on_device,
        mesh=mesh,
        in_specs=placed,
        out_specs=(
            P("batch", "seq", None),
            P("batch", "seq", None),
            P(("batch", "seq"), None),
            P(("batch", "seq"), None),
            P(("batch", "seq"), None),
            P(None, ("batch", "seq")),
            P(("batch", "seq"), None),
            P(("batch", "seq")),
            P(("batch", "seq"), None),
            P(("batch", "seq"), None),
            P(None, ("batch", "seq")),
            P(("batch", "seq")),
            P(),
        ),
        check_vma=False,
    )
```

profile of v0, /device:TPU:0, one launch (start us, length us, event | category | flops | bytes accessed | tf_op | source)
XLA Modules:
  0.0 2280.2 jit_solution(3998142124831837100)
XLA Ops:
  10.5 42.1 %all-reduce.5 = (bf16[2048]{0:T(1024)(128)(2,1)S(1)}, bf16[2048]{0:T(1024)(128)(2,1)S(1)}) all-reduce(bf16[2048]{0:T(1024)(128)(2,1)S(1)} %dynamic-update-slice, bf16[2048]{0:T(1024)(128)(2,1)S(1)} %dynamic-update-slice.1), channel_id=1, replica_groups=mesh['batch'=4,'seq'=8] {'batch','seq'}, use_global_device_ids=true, to_apply=%add | all-reduce | flops 4096 | bytes 16384
  57.6 41.2 %all-gather.4 = bf16[32,64,3]{1,2,0:T(4,128)(2,1)S(1)} all-gather(bf16[1,64,3]{1,2,0:T(4,128)(2,1)S(1)} %bitcast.312), channel_id=1, replica_groups=mesh['batch'=4,'seq'=8] {'batch','seq'}, dimensions={0}, use_global_device_ids=true | all-gather | bytes 12672 | tf_op jit(solution)/shard_map/all_gather | solution.py:145
  106.9 39.9 %all-gather.17.cloned.1.call-done = bf16[2048,2048]{1,0:T(8,128)(2,1)} async-done(((bf16[64,2048]{1,0:T(8,128)(2,1)}), bf16[2048,2048]{1,0:T(8,128)(2,1)}) %all-gather.17.cloned.1.call-update) | async-done | bytes 8388624 | tf_op jit(solution)/shard_map/all_gather | solution.py:143
  159.3 42.9 %all-gather.19.cloned.1.call-done = bf16[2048,256]{1,0:T(8,128)(2,1)} async-done(((bf16[64,256]{1,0:T(8,128)(2,1)}), bf16[2048,256]{1,0:T(8,128)(2,1)}) %all-gather.19.cloned.1.call-update) | async-done | bytes 1048592 | tf_op jit(solution)/shard_map/all_gather | solution.py:141
  203.7 15.8 all-gather.1
  227.8 283.4 %all-gather.35.cloned.1.call-done = f32[16,16,273,128]{3,1,2,0:T(8,128)} async-done(((f32[2,16,273,128]{3,1,2,0:T(8,128)}), f32[16,16,273,128]{3,1,2,0:T(8,128)}) %all-gather.35.cloned.1.call-update) | async-done | bytes 35782672 | tf_op jit(solution)/shard_map/all_gather | solution.py:25
  515.7 9.3 fusion.83
  527.7 62.8 %all-gather.23.cloned.1.call-done = bf16[2048,2048]{0,1:T(8,128)(2,1)} async-done(((bf16[2048,64]{0,1:T(8,128)(2,1)}), bf16[2048,2048]{0,1:T(8,128)(2,1)}) %all-gather.23.cloned.1.call-update) | async-done | bytes 8388624 | tf_op jit(solution)/shard_map/all_gather | solution.py:144
  601.7 46.9 %all_to_all.96 = bf16[64,8,688]{2,0,1:T(8,128)(2,1)} all-to-all(bf16[64,8,688]{2,0,1:T(8,128)(2,1)S(1)} %copy.162), channel_id=1, replica_groups=mesh['batch'=4,'seq'=8] {'seq'}, dimensions={1} | all-to-all | bytes 1409024 | tf_op jit(solution)/shard_map/all_to_all | solution.py:199
  651.2 44.1 %all_to_all.97 = bf16[64,8,688]{2,0,1:T(8,128)(2,1)} all-to-all(bf16[64,8,688]{2,0,1:T(8,128)(2,1)S(1)} %copy.163), channel_id=1, replica_groups=mesh['batch'=4,'seq'=8] {'seq'}, dimensions={1} | all-to-all | bytes 1409024 | tf_op jit(solution)/shard_map/all_to_all | solution.py:200
  698.1 35.8 %all_to_all.98 = bf16[64,8,688]{2,0,1:T(8,128)(2,1)} all-to-all(bf16[64,8,688]{2,0,1:T(8,128)(2,1)S(1)} %copy.164), channel_id=1, replica_groups=mesh['batch'=4,'seq'=8] {'seq'}, dimensions={1} | all-to-all | bytes 1409024 | tf_op jit(solution)/shard_map/all_to_all | solution.py:201
  734.0 16.6 copy.166
  750.6 13.2 reshape.287
  763.7 27.7 %all-gather.25.cloned.1.call-done = bf16[1024,2,2048]{2,1,0:T(2,128)(2,1)} async-done(((bf16[128,2,2048]{2,1,0:T(2,128)(2,1)}), bf16[1024,2,2048]{2,1,0:T(2,128)(2,1)}) %all-gather.25.cloned.1.call-update) | async-done | bytes 8388624 | tf_op jit(solution)/shard_map/all_gather | solution.py:211
  791.4 13.2 reshape.281
  804.6 31.2 %all-gather.27.cloned.1.call-done = bf16[2048,688]{1,0:T(8,128)(2,1)} async-done(((bf16[512,688]{1,0:T(8,128)(2,1)}), bf16[2048,688]{1,0:T(8,128)(2,1)}) %all-gather.27.cloned.1.call-update) | async-done | bytes 2818064 | tf_op jit(solution)/shard_map/all_gather | solution.py:204
  835.8 11.0 fusion.84
  846.8 34.9 %all-gather.29.cloned.1.call-done = bf16[2048,688]{1,0:T(8,128)(2,1)} async-done(((bf16[512,688]{1,0:T(8,128)(2,1)}), bf16[2048,688]{1,0:T(8,128)(2,1)}) %all-gather.29.cloned.1.call-update) | async-done | bytes 2818064 | tf_op jit(solution)/shard_map/all_gather | solution.py:205
  881.7 11.0 fusion.85
  892.7 34.7 %all-gather.31.cloned.1.call-done = bf16[2048,688]{1,0:T(8,128)(2,1)} async-done(((bf16[512,688]{1,0:T(8,128)(2,1)}), bf16[2048,688]{1,0:T(8,128)(2,1)}) %all-gather.31.cloned.1.call-update) | async-done | bytes 2818064 | tf_op jit(solution)/shard_map/all_gather | solution.py:206
  927.4 16.7 multiply_convert_fusion
  944.1 12.4 fusion.86
  956.4 13.2 add_convert_fusion
  969.7 14.1 convert_element_type.204
  983.8 10.5 copy.167
  994.4 11.8 convolution_convert_fusion
  1006.2 14.1 convert_element_type.199
  1020.4 10.8 copy.165
  1031.2 52.9 %reduce-scatter.15.cloned.1.call-done = bf16[128,2,2048]{2,0,1:T(8,128)(2,1)} async-done(((bf16[1024,2,2048]{2,0,1:T(8,128)(2,1)}), bf16[128,2,2048]{2,0,1:T(8,128)(2,1)}) %reduce-scatter.15.cloned.1.call-update) | async-done | bytes 1048592 | tf_op jit(solution)/shard_map/reduce_scatter | solution.py:235
  1086.6 87.6 %reduce-scatter.13.cloned.1.call-done = bf16[128,2,2048]{2,0,1:T(8,128)(2,1)} async-done(((bf16[1024,2,2048]{2,0,1:T(8,128)(2,1)}), bf16[128,2,2048]{2,0,1:T(8,128)(2,1)}) %reduce-scatter.13.cloned.1.call-update) | async-done | bytes 1048592 | tf_op jit(solution)/shard_map/reduce_scatter | solution.py:219
  1196.5 10.4 convolution_convert_fusion.2
  1207.0 10.9 convolution_convert_fusion.1
  1218.0 10.4 fusion.5
  1250.7 23.9 %all-gather.3 = bf16[16,16,273]{2,1,0:T(8,128)(2,1)} all-gather(bf16[2,16,273]{2,1,0:T(8,128)(2,1)S(1)} %bitcast.301), channel_id=5, replica_groups=mesh['batch'=4,'seq'=8] {'seq'}, dimensions={0}, use_global_device_ids=true | all-gather | bytes 157248 | tf_op jit(solution)/shard_map/all_gather | solution.py:39
  1274.6 8.0 fusion.4
  1287.6 69.1 %all-gather.37.cloned.1.call-done = bf16[16,16,273,128]{3,1,2,0:T(8,128)(2,1)} async-done(((bf16[2,16,273,128]{3,1,2,0:T(8,128)(2,1)}), bf16[16,16,273,128]{3,1,2,0:T(8,128)(2,1)}) %all-gather.37.cloned.1.call-update) | async-done | bytes 17891344 | tf_op jit(solution)/shard_map/all_gather | solution.py:39
  1356.7 61.0 %while.31 = (s32[]{:T(128)}, f32[2,16,273,128]{3,2,1,0:T(8,128)}, f32[2,16,273]{2,1,0:T(8,128)S(1)}, s32[]{:T(128)}, bf16[8,2,16,273,128]{4,2,3,1,0:T(8,128)(2,1...) while((s32[]{:T(128)}, f32[2,16,273,128]{3,2,1,0:T(8,128)}, ...), condition=%wide.region_13.14_spmd.clone, body=%wide.region_12.13_spmd.clone.sunk | while | flops 4507784 | bytes 15742449 | solution.py:57
  1452.4 9.8 fusion.33
  1464.1 9.3 fusion.29
  1482.5 19.2 all-to-all-done.3
  1508.3 20.2 all-to-all-done.4
  1545.6 10.0 all-to-all-done.5
  1561.9 38.8 %all-reduce.4 = (f32[2048]{0:T(1024)S(1)}, f32[2048]{0:T(1024)S(1)}, f32[]{:T(128)}) all-reduce(f32[2048]{0:T(1024)S(1)} %get-tuple-element.259, f32[2048]{0:T(1024)S(1)} %copy-done.50, f32[]{:T(128)} %get-tuple-element.293), channel_id=13, replica_groups=mesh['batch'=4,'seq'=8] {'batch','seq'}, use_global_device_ids=true, to_apply=%region_26.27.clone | all-reduce | flops 4097 | bytes 32776
  1606.0 20.8 reduce-scatter.31.cloned.1.call-done
  1628.2 134.3 %reduce-scatter.17.cloned.1.call-done = f32[64,256]{1,0:T(8,128)} async-done(((f32[2048,256]{1,0:T(8,128)}), f32[64,256]{1,0:T(8,128)}) %reduce-scatter.17.cloned.1.call-update) | async-done | bytes 65552 | tf_op jit(solution)/shard_map/reduce_scatter | solution.py:326
  1762.5 185.8 %reduce-scatter.23.cloned.1.call-done = f32[2048,64]{0,1:T(8,128)} async-done(((f32[2048,2048]{0,1:T(8,128)}), f32[2048,64]{0,1:T(8,128)}) %reduce-scatter.23.cloned.1.call-update) | async-done | bytes 524304 | tf_op jit(solution)/shard_map/reduce_scatter | solution.py:329
  1948.3 137.7 %reduce-scatter.19.cloned.1.call-done = f32[64,256]{1,0:T(8,128)} async-done(((f32[2048,256]{1,0:T(8,128)}), f32[64,256]{1,0:T(8,128)}) %reduce-scatter.19.cloned.1.call-update) | async-done | bytes 65552 | tf_op jit(solution)/shard_map/reduce_scatter | solution.py:327
  2086.0 185.9 %reduce-scatter.21.cloned.1.call-done = f32[64,2048]{1,0:T(8,128)} async-done(((f32[2048,2048]{1,0:T(8,128)}), f32[64,2048]{1,0:T(8,128)}) %reduce-scatter.21.cloned.1.call-update) | async-done | bytes 524304 | tf_op jit(solution)/shard_map/reduce_scatter | solution.py:328
  (319 shorter events, 255.3 us)
Async XLA Ops:
  7.2 92.7 %all-gather.21.cloned.1.call-start = ((), (), s32[]{:S(2)}) async-start(), calls=%async_computation.18 | async-start | bytes 1081344 | tf_op jit(solution)/shard_map/all_gather | solution.py:142
  7.9 49.7 %copy-start.57 = (bf16[64,3]{0,1:T(4,128)(2,1)S(1)}, bf16[64,3]{0,1:T(4,128)(2,1)}, u32[]{:S(2)}) copy-start(bf16[64,3]{0,1:T(4,128)(2,1)} %param.23) | copy-start | bytes 1156
  7.9 138.9 %all-gather.17.cloned.1.call-start = ((), (), s32[]{:S(2)}) async-start(), calls=%async_computation.16 | async-start | bytes 8650752 | tf_op jit(solution)/shard_map/all_gather | solution.py:143
  8.7 90.3 %copy-start.60 = (s32[8]{0:T(128)S(1)}, s32[8]{0:T(128)}, u32[]{:S(2)}) copy-start(s32[8]{0:T(128)} %param.18) | copy-start | bytes 100
  8.7 193.6 %all-gather.19.cloned.1.call-start = ((), (), s32[]{:S(2)}) async-start(), calls=%async_computation.17 | async-start | bytes 1081344 | tf_op jit(solution)/shard_map/all_gather | solution.py:141
  56.1 46.4 %copy-start.7 = (f32[2,128,2048]{2,1,0:T(8,128)}, f32[2,128,2048]{2,1,0:T(8,128)S(1)}, u32[]{:S(2)}) copy-start(f32[2,128,2048]{2,1,0:T(8,128)S(1)} %fusion.21) | copy-start | bytes 6291460
  56.2 43.0 %collective-permute-start = (bf16[2,2,2048]{2,1,0:T(2,128)(2,1)S(1)}, bf16[2,2,2048]{2,1,0:T(2,128)(2,1)S(1)}, u32[]{:S(2)}, u32[]{:S(2)}) collective-permute-start(bf16[2,2,2048]{2,1,0:T(2,128)(2,1)S(1)} %slice.81), channel_id=1, source_target_pairs={{0,1},{1,2},{2,3},{3,4},{4,5},{5,6},{6,7},{8,9},{9,10},{10,11},{11... | collective-permute-start | bytes 49160 | tf_op jit(solution)/shard_map/ppermute | solution.py:20
  57.5 453.7 %all-gather.35.cloned.1.call-start = ((), (), s32[]{:S(2)}) async-start(), calls=%async_computation.34 | async-start | bytes 40255488 | tf_op jit(solution)/shard_map/all_gather | solution.py:25
  99.2 415.9 %copy-start.51 = (f32[2,128]{1,0:T(2,128)}, f32[2,128]{1,0:T(2,128)S(1)}, u32[]{:S(2)}) copy-start(f32[2,128]{1,0:T(2,128)S(1)} %compare_convert_fusion) | copy-start | bytes 3076
  99.9 119.6 %copy-start.12 = (bf16[2,128,2048]{2,1,0:T(8,128)(2,1)}, bf16[2,128,2048]{2,1,0:T(8,128)(2,1)S(1)}, u32[]{:S(2)}) copy-start(bf16[2,128,2048]{2,1,0:T(8,128)(2,1)S(1)} %add_convert_fusion.1) | copy-start | bytes 3145732
  106.9 45.9 %copy-start.3 = (bf16[2,128,16,273]{1,3,2,0:T(8,128)(2,1)}, bf16[2,128,16,273]{1,3,2,0:T(8,128)(2,1)S(1)}, u32[]{:S(2)}) copy-start(bf16[2,128,16,273]{1,3,2,0:T(8,128)(2,1)S(1)} %get-tuple-element.297) | copy-start | bytes 6709252
  158.0 432.4 %all-gather.23.cloned.1.call-start = ((), (), s32[]{:S(2)}) async-start(), calls=%async_computation.19 | async-start | bytes 8650752 | tf_op jit(solution)/shard_map/all_gather | solution.py:144
  158.6 575.4 %all-gather.33.cloned.1.call-start = ((), (), s32[]{:S(2)}) async-start(), calls=%async_computation.25 | async-start | bytes 9437184 | tf_op jit(solution)/shard_map/all_gather | solution.py:212
  159.2 632.2 %all-gather.25.cloned.1.call-start = ((), (), s32[]{:S(2)}) async-start(), calls=%async_computation.20 | async-start | bytes 9437184 | tf_op jit(solution)/shard_map/all_gather | solution.py:211
  159.3 64.4 %copy-start.25 = (f32[128,128]{0,1:T(8,128)}, f32[128,128]{0,1:T(8,128)S(1)}, u32[]{:S(2)}) copy-start(f32[128,128]{0,1:T(8,128)S(1)} %fusion.75) | copy-start | bytes 196612
  222.5 293.2 %copy-start.1 = (bf16[2,128,16,273]{1,3,2,0:T(8,128)(2,1)}, bf16[2,128,16,273]{1,3,2,0:T(8,128)(2,1)S(1)}, u32[]{:S(2)}) copy-start(bf16[2,128,16,273]{1,3,2,0:T(8,128)(2,1)S(1)} %pad_maximum_fusion) | copy-start | bytes 6709252
  515.7 9.3 copy-start.38
  515.7 74.7 %copy-start.17 = (bf16[2,128,2048]{2,1,0:T(8,128)(2,1)S(1)}, bf16[2,128,2048]{2,1,0:T(8,128)(2,1)}, u32[]{:S(2)}) copy-start(bf16[2,128,2048]{2,1,0:T(8,128)(2,1)} %param.17) | copy-start | bytes 3145732
  599.0 236.8 %all-gather.27.cloned.1.call-start = ((), (), s32[]{:S(2)}) async-start(), calls=%async_computation.21 | async-start | bytes 3932160 | tf_op jit(solution)/shard_map/all_gather | solution.py:204
  648.6 233.1 %all-gather.29.cloned.1.call-start = ((), (), s32[]{:S(2)}) async-start(), calls=%async_computation.22 | async-start | bytes 3932160 | tf_op jit(solution)/shard_map/all_gather | solution.py:205
  695.4 232.0 %all-gather.31.cloned.1.call-start = ((), (), s32[]{:S(2)}) async-start(), calls=%async_computation.23 | async-start | bytes 3932160 | tf_op jit(solution)/shard_map/all_gather | solution.py:206
  733.9 350.2 %reduce-scatter.15.cloned.1.call-start = ((), (), s32[]{:S(2)}) async-start(), calls=%async_computation.26 | async-start | bytes 9437184 | tf_op jit(solution)/shard_map/reduce_scatter | solution.py:235
  927.4 16.7 copy-start.58
  944.1 12.4 copy-start.59
  994.4 179.9 %reduce-scatter.13.cloned.1.call-start = ((), (), s32[]{:S(2)}) async-start(), calls=%async_computation.24 | async-start | bytes 9437184 | tf_op jit(solution)/shard_map/reduce_scatter | solution.py:219
  1031.1 143.2 %copy-start.34 = (bf16[2,128,2048]{2,1,0:T(8,128)(2,1)S(1)}, bf16[2,128,2048]{2,1,0:T(8,128)(2,1)}, u32[]{:S(2)}) copy-start(bf16[2,128,2048]{2,1,0:T(8,128)(2,1)} %param.29) | copy-start | bytes 3145732
  1031.1 325.6 %all-gather.37.cloned.1.call-start = ((), (), s32[]{:S(2)}) async-start(), calls=%async_computation.35 | async-start | bytes 20127744 | tf_op jit(solution)/shard_map/all_gather | solution.py:39
  1177.7 6.5 copy-start.9
  1196.4 277.0 %reduce-scatter.25.cloned.1.call-start = ((), (), s32[]{:S(2)}) async-start(), calls=%async_computation.31 | async-start | bytes 3522560 | tf_op jit(solution)/shard_map/reduce_scatter | solution.py:245
  1206.9 273.3 %reduce-scatter.27.cloned.1.call-start = ((), (), s32[]{:S(2)}) async-start(), calls=%async_computation.32 | async-start | bytes 3522560 | tf_op jit(solution)/shard_map/reduce_scatter | solution.py:248
  1217.9 288.1 %reduce-scatter.29.cloned.1.call-start = ((), (), s32[]{:S(2)}) async-start(), calls=%async_computation.33 | async-start | bytes 3522560 | tf_op jit(solution)/shard_map/reduce_scatter | solution.py:251
  1228.4 398.4 %reduce-scatter.31.cloned.1.call-start = ((), (), s32[]{:S(2)}) async-start(), calls=%async_computation.36 | async-start | bytes 1081344
  1238.9 35.6 %slice-start.2 = ((s8[4587520]{0:T(1024)(128)(4,1)}), s8[4194304]{0:T(1024)(128)(4,1)S(1)}, s32[]{:S(2)}) async-start(s8[4587520]{0:T(1024)(128)(4,1)} %bitcast.248), calls=%async_computation.39 | async-start | bytes 8388608
  1242.9 31.6 %slice-start.3 = ((s8[4587520]{0:T(1024)(128)(4,1)}), s8[393216]{0:T(1024)(128)(4,1)S(1)}, s32[]{:S(2)}) async-start(s8[4587520]{0:T(1024)(128)(4,1)} %bitcast.248), calls=%async_computation.40 | async-start | bytes 786432
  1248.6 25.9 %copy-start.36 = (f32[2,16,273]{2,1,0:T(8,128)S(1)}, f32[2,16,273]{2,1,0:T(8,128)}, u32[]{:S(2)}) copy-start(f32[2,16,273]{2,1,0:T(8,128)} %copy-done.35) | copy-start | bytes 104836
  1356.7 61.0 %copy-start.52 = (f32[2,128]{1,0:T(2,128)S(1)}, f32[2,128]{1,0:T(2,128)}, u32[]{:S(2)}) copy-start(f32[2,128]{1,0:T(2,128)} %copy-done.51) | copy-start | bytes 3076
  1435.1 6.3 copy-start.33
  1442.0 3.3 collective-permute-start.1
  1450.4 312.1 %reduce-scatter.17.cloned.1.call-start = ((), (), s32[]{:S(2)}) async-start(), calls=%async_computation.27 | async-start | bytes 2162688 | tf_op jit(solution)/shard_map/reduce_scatter | solution.py:326
  1452.3 495.9 %reduce-scatter.23.cloned.1.call-start = ((), (), s32[]{:S(2)}) async-start(), calls=%async_computation.30 | async-start | bytes 17301504 | tf_op jit(solution)/shard_map/reduce_scatter | solution.py:329
  1462.2 623.8 %reduce-scatter.19.cloned.1.call-start = ((), (), s32[]{:S(2)}) async-start(), calls=%async_computation.28 | async-start | bytes 2162688 | tf_op jit(solution)/shard_map/reduce_scatter | solution.py:327
  1464.1 807.8 %reduce-scatter.21.cloned.1.call-start = ((), (), s32[]{:S(2)}) async-start(), calls=%async_computation.29 | async-start | bytes 17301504 | tf_op jit(solution)/shard_map/reduce_scatter | solution.py:328
  1475.7 25.9 %all-to-all-start.3 = ((bf16[8,64,688]{2,1,0:T(8,128)(2,1)}), bf16[8,64,688]{2,1,0:T(8,128)(2,1)S(1)}, u32[]{:S(2)}, u32[]{:S(2)}) async-start(bf16[8,64,688]{2,1,0:T(8,128)(2,1)} %bitcast.61), calls=%async_computation.10 | async-start | bytes 1572864 | tf_op jit(solution)/shard_map/all_to_all | solution.py:256
  1501.7 31.3 %copy-start.61 = (s32[8]{0:T(128)S(1)}, s32[8]{0:T(128)}, u32[]{:S(2)}) copy-start(s32[8]{0:T(128)} %param.18) | copy-start | bytes 100
  1501.7 26.8 %all-to-all-start.4 = ((bf16[8,64,688]{2,1,0:T(8,128)(2,1)}), bf16[8,64,688]{2,1,0:T(8,128)(2,1)}, u32[]{:S(2)}, u32[]{:S(2)}) async-start(bf16[8,64,688]{2,1,0:T(8,128)(2,1)} %bitcast.63), calls=%async_computation.12 | async-start | bytes 1572864 | tf_op jit(solution)/shard_map/all_to_all | solution.py:259
  1528.5 27.1 %all-to-all-start.5 = ((bf16[8,64,688]{2,1,0:T(8,128)(2,1)}), bf16[8,64,688]{2,1,0:T(8,128)(2,1)}, u32[]{:S(2)}, u32[]{:S(2)}) async-start(bf16[8,64,688]{2,1,0:T(8,128)(2,1)} %bitcast.66), calls=%async_computation.14 | async-start | bytes 1572864 | tf_op jit(solution)/shard_map/all_to_all | solution.py:262
  1558.9 43.6 %copy-start.56 = (f32[2,128]{1,0:T(2,128)S(1)}, f32[2,128]{1,0:T(2,128)}, u32[]{:S(2)}) copy-start(f32[2,128]{1,0:T(2,128)} %copy-done.55) | copy-start | bytes 3076
  1558.9 43.6 %copy-start.19 = (bf16[2,128,2048]{2,1,0:T(8,128)(2,1)S(1)}, bf16[2,128,2048]{2,1,0:T(8,128)(2,1)}, u32[]{:S(2)}) copy-start(bf16[2,128,2048]{2,1,0:T(8,128)(2,1)} %param.17) | copy-start | bytes 3145732
  (43 other events, 121.7 us)
Sparse Core Ops, SparseCore 0:
  11.0 56.4 all-gather.20
  70.5 76.2 all-gather.16
  149.8 52.3 all-gather.18
  203.7 307.3 all-gather.34
  514.0 76.3 all-gather.22
  591.9 114.0 all-gather.32
  708.2 83.2 all-gather.24
  793.3 42.4 all-gather.26
  837.6 43.9 all-gather.28
  883.3 43.9 all-gather.30
  994.5 89.5 reduce-scatter.14
  1086.3 87.9 reduce-scatter.12
  1196.5 160.1 all-gather.36
  1359.6 39.4 reduce-scatter.24
  1402.0 41.2 reduce-scatter.26
  1446.1 41.1 reduce-scatter.28
  1489.5 137.2 reduce-scatter.30
  1629.6 132.9 reduce-scatter.16
  1765.4 182.8 reduce-scatter.22
  1951.0 134.9 reduce-scatter.18
  2088.9 182.8 reduce-scatter.20
where the time goes:
time: 2290 us; the launch traced here: 2280 us
  waiting for transfers between devices  1490 us (65%)
  blocking collectives  289 us (13%)
  matrix products  221 us (10%)
  local copies, waits for them, and re-layouts  174 us (8%)
  other arithmetic  75.4 us (3%)
    all_gather x1, waiting for transfers between devices, carried_in(): gathered = jax.tree.map(lambda a: lax.all_gather(a, axis), part)  283 us
    reduce_scatter x1, waiting for transfers between devices, on_device(): lax.psum_scatter(grad_v_full, ('batch', 'seq'), scatter_dimension=0, tile...  186 us
    reduce_scatter x1, waiting for transfers between devices, on_device(): lax.psum_scatter(grad_out_full, ('batch', 'seq'), scatter_dimension=1, ti...  186 us
    reduce_scatter x1, waiting for transfers between devices, on_device(): lax.psum_scatter(grad_k_full, ('batch', 'seq'), scatter_dimension=0, tile...  138 us
    reduce_scatter x1, waiting for transfers between devices, on_device(): lax.psum_scatter(grad_q_full, ('batch', 'seq'), scatter_dimension=0, tile...  134 us
    reduce_scatter x1, waiting for transfers between devices, on_device(): lax.psum_scatter(back_product(hidden_act, down_cols).reshape(lax.axis_siz...  87.6 us
    unnamed x2, blocking collectives  80.9 us
    all_gather x1, waiting for transfers between devices, entering(): lax.all_gather(part.astype(kind), axis)  69.1 us
  transfers between devices with their start and end apart: 26, of which 20 were waited for; matrix products, arithmetic and copies ran while one was open for 16% of the time, Pallas kernels for 0%

commit v1 on v0

v1 whole, which is shorter than its diff:
```python
import math

import jax
import jax.numpy as jnp
import ml_dtypes
from jax import lax
from jax.experimental import pallas as pl
from jax.experimental.pallas import tpu as pltpu
from jax.sharding import PartitionSpec as P

HEADS = 16
FEAT = 16
KERNEL = 3
LANES = 128
HALF = 64

epsilon = 1e-06
bf16 = jnp.bfloat16
f32 = jnp.float32
alpha = (2.0 * FEAT) ** -0.25
shift = math.sqrt(FEAT) / math.sqrt(2.0 * FEAT)


def rms_norm(v, gain):
    return v * lax.rsqrt(jnp.mean(v * v, axis=-1, keepdims=True) + epsilon) * gain


def contract(left, right, dims, kind=f32):
    return lax.dot_general(left, right, ((dims[:1], dims[1:]), ((), ())), preferred_element_type=kind)


def nn(left, right):
    return contract(left, right, (1, 0))


def nt(left, right):
    return contract(left, right, (1, 1))


def tn(left, right):
    return contract(left, right, (0, 0))


def pick(value, at, axis=0):
    return lax.dynamic_index_in_dim(value, at, axis, False)


class Links:
    def __init__(self):
        self.nb, self.ns = (lax.axis_size("batch"), lax.axis_size("seq"))
        self.nz = self.ns // 2
        self.b = lax.axis_index("batch")
        seq = lax.axis_index("seq")
        self.z, self.c = (seq // 2, seq % 2)
        self.seq = seq

    def core(self, value):
        return lax.ppermute(value, "seq", [(s, s ^ 1) for s in range(self.ns)])

    def ring(self, value):
        return lax.ppermute(value, "seq", [(s, (s + 2) % self.ns) for s in range(self.ns)])

    def across(self, value, d):
        return lax.ppermute(value, "batch", [(b, b ^ d) for b in range(self.nb)])

    def to_seq(self, value, dz, dc):
        return lax.ppermute(
            value,
            "seq",
            [(s, 2 * ((s // 2 + dz) % self.nz) + ((s % 2) ^ dc)) for s in range(self.ns)],
        )

    def behind(self, k):
        return lax.rem(self.z + (self.nz - k), self.nz)

    def gather_plane(self, x):
        h = x.shape[0] // 2
        one, two = (self.across(x, 1), self.across(x, 2))
        three = (self.across(one[:h], 2), self.across(two[h:], 1))
        mine = (x, one, two) + three
        return jnp.concatenate(mine + tuple(self.core(v) for v in mine), axis=0)

    def scatter_plane(self, part):
        s = part[0].astype(f32) + self.core(part[1]).astype(f32)
        h = s.shape[1] // 2
        far = s[3].astype(bf16)
        a, b = (self.across(far[:h], 1), self.across(far[h:], 2))
        to_two = jnp.concatenate([s[2, :h] + a.astype(f32), s[2, h:]], axis=0).astype(bf16)
        to_one = jnp.concatenate([s[1, :h], s[1, h:] + b.astype(f32)], axis=0).astype(bf16)
        return s[0] + self.across(to_one, 1).astype(f32) + self.across(to_two, 2).astype(f32)

    def gather_all(self, x):
        chain = [x]
        for _ in range(self.nz - 1):
            chain.append(self.ring(chain[-1]))
        column = jnp.stack(chain)
        h = self.nz // 2
        one, two = (self.across(column, 1), self.across(column, 2))
        mine = (
            (column, 0, 0),
            (one, 1, 0),
            (two, 2, 0),
            (self.across(one[:h], 2), 3, 0),
            (self.across(two[h:], 1), 3, h),
        )
        items, places = ([], [])
        for dc in range(2):
            for value, d, first in mine:
                got = self.core(value) if dc else value
                for k in range(value.shape[0]):
                    items.append((got, k))
                    places.append((self.behind(first + k) * self.nb + (self.b ^ d)) * 2 + (self.c ^ dc))
        return items, places

    def scatter_all(self, part):
        kind = part.dtype
        got = self.core(pick(part, self.c ^ 1, 2))
        pair = (pick(part, self.c, 2).astype(f32) + got.astype(f32)).astype(kind)
        h = self.nz // 2
        s = [pick(pair, self.b ^ d, 1) for d in range(4)]
        a, b = (self.across(s[3][:h], 1), self.across(s[3][h:], 2))
        to_two = jnp.concatenate([(s[2][:h].astype(f32) + a.astype(f32)).astype(kind), s[2][h:]], axis=0)
        to_one = jnp.concatenate([s[1][:h], (s[1][h:].astype(f32) + b.astype(f32)).astype(kind)], axis=0)
        line = (
            s[0].astype(f32) + self.across(to_one, 1).astype(f32) + self.across(to_two, 2).astype(f32)
        ).astype(kind)
        return self.scatter_ring([pick(line, self.behind(j)) for j in range(self.nz)])

    def scatter_ring(self, parts):
        total = parts[1 % self.nz].astype(f32)
        for j in range(1, self.nz):
            total = self.ring(total.astype(parts[0].dtype)).astype(f32) + parts[(j + 1) % self.nz].astype(f32)
        return total

    def exchange_seq(self, value):
        got, sources = ([], [])
        for dz in range(self.nz):
            for dc in range(2):
                to = 2 * lax.rem(self.z + dz, self.nz) + (self.c ^ dc)
                piece = pick(value, to)
                got.append(self.to_seq(piece, dz, dc) if dz or dc else piece)
                sources.append(2 * self.behind(dz) + (self.c ^ dc))
        return got, sources

    def sum_all(self, value):
        value = value + self.core(value)
        value = value + self.across(value, 1)
        value = value + self.across(value, 2)
        moving = value
        for _ in range(self.nz - 1):
            moving = self.ring(moving)
            value = value + moving
        return value


def assemble(items, places, shape, view):
    arrays, plan = ([], [])
    for value, at in items:
        known = [i for i, a in enumerate(arrays) if a is value]
        if not known:
            arrays.append(value)
            known = [len(arrays) - 1]
        plan.append((known[0], at))
    count = len(arrays)

    def kernel(place, *refs):
        out, sems = (refs[count], refs[count + 1])
        copies = []
        for t, (i, at) in enumerate(plan):
            source = refs[i] if at is None else refs[i].at[at]
            copies.append(pltpu.make_async_copy(source, view(out, place[t]), sems.at[t]))
            copies[-1].start()
        for copy in copies:
            copy.wait()

    size = math.prod(shape)
    return pl.pallas_call(
        kernel,
        out_shape=jax.ShapeDtypeStruct(shape, arrays[0].dtype),
        in_specs=[pl.BlockSpec(memory_space=pltpu.SMEM)] + [pl.BlockSpec(memory_space=pl.ANY)] * count,
        out_specs=pl.BlockSpec(memory_space=pltpu.VMEM),
        scratch_shapes=[pltpu.SemaphoreType.DMA((len(plan),))],
        compiler_params=pltpu.CompilerParams(vmem_limit_bytes=40 * 1024 * 1024),
        cost_estimate=pl.CostEstimate(flops=0, bytes_accessed=4 * size, transcendentals=0),
    )(jnp.stack(places).astype(jnp.int32), *arrays)


def join_rows(items, places, rows, width):
    return assemble(
        items,
        places,
        (len(items) * rows, width),
        lambda out, at: out.at[pl.ds(pl.multiple_of(at * rows, rows), rows)],
    )


def join_lead(parts, places):
    return assemble(
        [(p, None) for p in parts],
        places,
        (len(parts),) + parts[0].shape,
        lambda out, at: out.at[at],
    )


def join_lanes(parts, places):
    width = parts[0].shape[-1]
    if width % LANES:
        whole = jnp.moveaxis(join_lead(parts, places), 0, -2)
        return whole.reshape(whole.shape[:-2] + (len(parts) * width,))
    return assemble(
        [(p, None) for p in parts],
        places,
        parts[0].shape[:-1] + (len(parts) * width,),
        lambda out, at: out.at[:, :, pl.ds(pl.multiple_of(at * width, width), width)],
    )


def sweep(lower, upper, body):
    if isinstance(lower, int) and isinstance(upper, int) and upper - lower <= 4:
        for i in range(lower, upper):
            body(i)
    else:
        lax.fori_loop(lower, upper, lambda i, none: (body(i), none)[1], None)


def rows_at(i, block):
    return pl.ds(i * block if isinstance(i, int) else pl.multiple_of(i * block, block), block)


def lane_of(shape):
    return lax.broadcasted_iota(jnp.int32, shape, 1)


def fetch(places, pieces, target, sems, first, rows):
    copies = []
    for t, piece in enumerate(pieces):
        copies.append(
            pltpu.make_async_copy(
                piece,
                target.at[pl.ds(pl.multiple_of(places[t] * rows, rows), rows)],
                sems.at[first + t],
            )
        )
        copies[-1].start()
    return copies


def prepare(i, block, units, length, qkv, qa, ka, va):
    rows = rows_at(i, block)
    raw = qkv[rows, :LANES].astype(f32)
    lane = lane_of((block, LANES))
    valid = (i * block + lax.broadcasted_iota(jnp.int32, (block, LANES), 0)) < length
    high = float(ml_dtypes.bfloat16(shift))
    keys = jnp.where(
        lane < HALF,
        pltpu.roll(raw, HALF, 1),
        jnp.where(lane == HALF, high, jnp.where(lane == HALF + 1, shift - high, 0.0)),
    )
    ka[rows, :] = jnp.where(valid, keys, 0.0).astype(bf16)
    extra = jnp.where((lane == HALF) | (lane == HALF + 1), 1.0, 0.0)
    ones = jnp.where(valid & (lane < 2), 1.0, 0.0).astype(bf16)
    for u in range(units):
        own = (lane >= u * FEAT) & (lane < (u + 1) * FEAT)
        qa[u, rows, :] = jnp.where(own, raw, extra).astype(bf16)
        v = qkv[rows, pl.ds(LANES * (u + 1), LANES)]
        va[u, rows, :LANES] = jnp.where(valid, v.astype(f32), 0.0).astype(bf16)
        va[u, rows, LANES:] = ones


def lower_triangle(block):
    shape = (block, block)
    return lax.broadcasted_iota(jnp.int32, shape, 0) >= lax.broadcasted_iota(jnp.int32, shape, 1)


def upper_triangle(block):
    shape = (block, block)
    return lax.broadcasted_iota(jnp.int32, shape, 0) <= lax.broadcasted_iota(jnp.int32, shape, 1)


def attend(pieces, sources, length, units, block):
    count = len(pieces)
    rows_each = pieces[0].shape[0]
    total = count * rows_each
    blocks = total // block

    def kernel(places, length_ref, *refs):
        y, attn, den = refs[count : count + 3]
        qkv, qa, ka, va, sems = refs[count + 3 :]
        for copy in fetch(places, refs[:count], qkv, sems, 0, rows_each):
            copy.wait()
        valid_len = length_ref[0]
        sweep(0, blocks, lambda i: prepare(i, block, units, valid_len, qkv, qa, ka, va))

        def one(i):
            rows = rows_at(i, block)
            lane = lane_of((block, LANES))
            den_all = jnp.zeros((block, LANES), f32)
            for u in range(units):

                def term(j, masked=False):
                    s = nt(qa[u, rows, :], ka[rows_at(j, block), :])
                    p = s * s + 0.5
                    if masked:
                        p = jnp.where(lower_triangle(block), p, 0.0)
                    return nn(p.astype(bf16), va[u, rows_at(j, block), :])

                total_u = term(i, True)
                if isinstance(i, int):
                    for j in range(i):
                        total_u = total_u + term(j)
                else:
                    total_u = lax.fori_loop(0, i, lambda j, t: t + term(j), total_u)
                den_u = total_u[:, LANES : LANES + 1]
                out = total_u[:, :LANES] / den_u
                cols = pl.ds(LANES * u, LANES)
                attn[rows, cols] = out
                y[rows, cols] = out.astype(bf16)
                den_all = jnp.where(lane == u, den_u, den_all)
            den[rows, :] = den_all

        sweep(0, blocks, one)

    return pl.pallas_call(
        kernel,
        out_shape=(
            jax.ShapeDtypeStruct((total, LANES * units), bf16),
            jax.ShapeDtypeStruct((total, LANES * units), f32),
            jax.ShapeDtypeStruct((total, LANES), f32),
        ),
        in_specs=[pl.BlockSpec(memory_space=pltpu.SMEM)] * 2 + [pl.BlockSpec(memory_space=pl.ANY)] * count,
        out_specs=[pl.BlockSpec(memory_space=pltpu.VMEM)] * 3,
        scratch_shapes=[
            pltpu.VMEM((total, LANES * (units + 1)), bf16),
            pltpu.VMEM((units, total, LANES), bf16),
            pltpu.VMEM((total, LANES), bf16),
            pltpu.VMEM((units, total, 2 * LANES), bf16),
            pltpu.SemaphoreType.DMA((count,)),
        ],
        compiler_params=pltpu.CompilerParams(vmem_limit_bytes=48 * 1024 * 1024),
        cost_estimate=pl.CostEstimate(
            flops=units * total * total * 400, bytes_accessed=total * 4096, transcendentals=0
        ),
    )(jnp.stack(sources).astype(jnp.int32), length, *pieces)


def attend_back(pieces, sources, length, d_pieces, attn, den, units, block):
    count = len(pieces)
    rows_each = pieces[0].shape[0]
    total = count * rows_each
    blocks = total // block

    def kernel(places, length_ref, *refs):
        attn_ref, den_ref = refs[2 * count : 2 * count + 2]
        out = refs[2 * count + 2]
        qkv, qa, ka, va, dy, dna, dq, dk, dv, sems = refs[2 * count + 3 :]
        copies = fetch(places, refs[:count], qkv, sems, 0, rows_each)
        copies += fetch(places, refs[count : 2 * count], dy, sems, count, rows_each)
        for copy in copies:
            copy.wait()
        valid_len = length_ref[0]

        def ready(i):
            prepare(i, block, units, valid_len, qkv, qa, ka, va)
            rows = rows_at(i, block)
            lane = lane_of((block, LANES))
            for u in range(units):
                cols = pl.ds(LANES * u, LANES)
                inverse = 1.0 / den_ref[rows, u : u + 1]
                grad = dy[rows, cols].astype(f32)
                scaled = -jnp.sum(grad * attn_ref[rows, cols], axis=1, keepdims=True) * inverse
                high = scaled.astype(bf16).astype(f32)
                dna[u, rows, :LANES] = (grad * inverse).astype(bf16)
                dna[u, rows, LANES:] = jnp.where(
                    lane == 0, high, jnp.where(lane == 1, scaled - high, 0.0)
                ).astype(bf16)
            dq[rows, :] = jnp.zeros((block, LANES), f32)
            dk[rows, :] = jnp.zeros((block, LANES), f32)
            dv[rows, :] = jnp.zeros((block, LANES * units), f32)

        sweep(0, blocks, ready)

        def pair(i, j, masked):
            t_rows, s_rows = (rows_at(i, block), rows_at(j, block))
            lane = lane_of((block, LANES))
            for u in range(units):
                q, k, v, g = (qa[u, t_rows, :], ka[s_rows, :], va[u, s_rows, :], dna[u, t_rows, :])
                ds = nt(g, v) * nt(q, k)
                if masked:
                    ds = jnp.where(lower_triangle(block), ds, 0.0)
                own = (lane >= u * FEAT) & (lane < (u + 1) * FEAT)
                dq[t_rows, :] += jnp.where(own, nn(ds.astype(bf16), k), 0.0)
                s_t = nt(k, q)
                ds_t = nt(v, g) * s_t
                p_t = s_t * s_t + 0.5
                if masked:
                    ds_t = jnp.where(upper_triangle(block), ds_t, 0.0)
                    p_t = jnp.where(upper_triangle(block), p_t, 0.0)
                dk[s_rows, :] += nn(ds_t.astype(bf16), q)
                dv[s_rows, pl.ds(LANES * u, LANES)] += nn(p_t.astype(bf16), g[:, :LANES])

        def one(j):
            pair(j, j, True)
            sweep(j + 1, blocks, lambda i: pair(i, j, False))

        sweep(0, blocks, one)

        def finish(i):
            rows = rows_at(i, block)
            lane = lane_of((block, LANES))
            valid = (i * block + lax.broadcasted_iota(jnp.int32, (block, LANES), 0)) < valid_len
            keys = jnp.where(valid & (lane < HALF), dk[rows, :], 0.0)
            both = jnp.where(lane < HALF, dq[rows, :], pltpu.roll(keys, HALF, 1))
            out[rows, :LANES] = (both * (2.0 * alpha)).astype(bf16)
            for u in range(units):
                grad = dv[rows, pl.ds(LANES * u, LANES)]
                out[rows, pl.ds(LANES * (u + 1), LANES)] = jnp.where(valid, grad, 0.0).astype(bf16)

        sweep(0, blocks, finish)

    return pl.pallas_call(
        kernel,
        out_shape=jax.ShapeDtypeStruct((total, LANES * (units + 1)), bf16),
        in_specs=[pl.BlockSpec(memory_space=pltpu.SMEM)] * 2
        + [pl.BlockSpec(memory_space=pl.ANY)] * (2 * count)
        + [pl.BlockSpec(memory_space=pltpu.VMEM)] * 2,
        out_specs=pl.BlockSpec(memory_space=pltpu.VMEM),
        scratch_shapes=[
            pltpu.VMEM((total, LANES * (units + 1)), bf16),
            pltpu.VMEM((units, total, LANES), bf16),
            pltpu.VMEM((total, LANES), bf16),
            pltpu.VMEM((units, total, 2 * LANES), bf16),
            pltpu.VMEM((total, LANES * units), bf16),
            pltpu.VMEM((units, total, 2 * LANES), bf16),
            pltpu.VMEM((total, LANES), f32),
            pltpu.VMEM((total, LANES), f32),
            pltpu.VMEM((total, LANES * units), f32),
            pltpu.SemaphoreType.DMA((2 * count,)),
        ],
        compiler_params=pltpu.CompilerParams(vmem_limit_bytes=56 * 1024 * 1024),
        cost_estimate=pl.CostEstimate(
            flops=units * total * total * 1200, bytes_accessed=total * 8192, transcendentals=0
        ),
    )(jnp.stack(sources).astype(jnp.int32), length, *pieces, *d_pieces, attn, den)


def weight_grad(links, left, right):
    tokens, width = left.shape
    block = right.shape[1] // links.nz

    def kernel(place, left_ref, right_ref, out_ref):
        out_ref[0] = tn(left_ref[...], right_ref[...]).astype(bf16)

    return pl.pallas_call(
        kernel,
        out_shape=jax.ShapeDtypeStruct((links.nz, width, block), bf16),
        grid_spec=pltpu.PrefetchScalarGridSpec(
            num_scalar_prefetch=1,
            grid=(links.nz,),
            in_specs=[
                pl.BlockSpec((tokens, width), lambda j, at: (0, 0)),
                pl.BlockSpec((tokens, block), lambda j, at: (0, at[j])),
            ],
            out_specs=pl.BlockSpec((1, width, block), lambda j, at: (j, 0, 0)),
        ),
        compiler_params=pltpu.CompilerParams(vmem_limit_bytes=56 * 1024 * 1024),
        cost_estimate=pl.CostEstimate(
            flops=2 * tokens * width * right.shape[1],
            bytes_accessed=2 * (tokens * width + right.size + width * right.shape[1]),
            transcendentals=0,
        ),
    )(jnp.stack([links.behind(j) for j in range(links.nz)]).astype(jnp.int32), left, right)


def on_device(
    hidden_in,
    lengths,
    q_weight,
    k_weight,
    v_weight,
    out_weight,
    conv_weight,
    norm_attn,
    gate_weight,
    up_weight,
    down_weight,
    norm_mlp,
    cotangent,
):
    links = Links()
    nb, nz, ns = (links.nb, links.nz, links.ns)
    rows, local, width = hidden_in.shape
    tokens = rows * local
    own = width // (nb * ns)
    groups = ns // rows
    units = HEADS // groups
    value_dim = width // HEADS
    lag = KERNEL - 1
    hidden_dim = gate_weight.shape[1]
    slice_dim = hidden_dim // (2 * nb)
    seq_len = local * ns

    def by_plane(v):
        return v.reshape(v.shape[:-1] + (nb, nz, 2 * own)).swapaxes(-3, -2).reshape(v.shape)

    def by_owner(v):
        return v.reshape(v.shape[:-1] + (nz, nb, 2 * own)).swapaxes(-3, -2).reshape(v.shape)

    own_lengths = lax.dynamic_slice_in_dim(lengths, links.b * rows, rows, 0)
    total_valid = jnp.sum(lengths).astype(f32)

    small = jnp.concatenate([norm_attn[None], norm_mlp[None], conv_weight.T], axis=0)
    items, places = links.gather_all(small)
    small_all = jnp.zeros((nz * nb * 2,) + small.shape, bf16)
    for (value, k), at in zip(items, places):
        small_all = lax.dynamic_update_slice_in_dim(small_all, value[k][None], at, 0)
    small_all = small_all.swapaxes(0, 1).reshape(small.shape[0], width).astype(f32)
    gain_attn, gain_mlp, taps = (small_all[0], small_all[1], small_all[2:])

    def paired(q_part, k_part):
        pad = ((0, 0), (0, 0), (0, HALF - units * FEAT))
        q_part = jnp.pad(q_part.reshape(-1, groups, units * FEAT), pad)
        k_part = jnp.pad(k_part.reshape(-1, groups, units * FEAT), pad)
        return jnp.concatenate([q_part, k_part], axis=-1).reshape(-1, groups * LANES)

    packed = jnp.concatenate([paired(q_weight, k_weight), v_weight], axis=1)
    w_in = join_rows(*links.gather_all(packed), own, packed.shape[1])
    w_out = join_rows(*links.gather_all(out_weight.T), own, width)

    x = by_plane(hidden_in)
    edge = lax.ppermute(x[:, local - lag :], "seq", [(s, s + 1) for s in range(ns - 1)])
    inputs = x.astype(f32)
    extended = rms_norm(jnp.concatenate([edge.astype(f32), inputs], axis=1), gain_attn)
    mixed = sum(taps[j] * extended[:, lag - j : lag - j + local] for j in range(KERNEL))
    c_low = mixed.astype(bf16).reshape(tokens, width)
    proj = nn(c_low, w_in)
    qk_width = groups * LANES
    qk = (proj[:, :qk_width] * alpha).astype(bf16).reshape(rows, local, groups, LANES)
    v_low = proj[:, qk_width:].astype(bf16).reshape(rows, local, groups, units * value_dim)
    outgoing = jnp.concatenate([qk, v_low], axis=-1).swapaxes(1, 2)
    outgoing = outgoing.reshape((ns, local, LANES * (units + 1)))
    pieces, sources = links.exchange_seq(outgoing)
    row_length = pick(own_lengths, links.seq // groups)
    block = min(256, seq_len)
    y_units, attn_units, den_units = attend(pieces, sources, row_length[None], units, block)
    y_pieces, y_sources = links.exchange_seq(y_units.reshape(ns, local, units * value_dim))

    def merge_heads(parts, froms):
        whole = join_lead(parts, froms).reshape(rows, groups, local, -1)
        return whole.swapaxes(1, 2).reshape(tokens, -1)

    y_low = merge_heads(y_pieces, y_sources)
    counted = (jnp.arange(seq_len, dtype=jnp.int32) < row_length)[:, None]
    den_sum = jnp.sum(jnp.where(counted, den_units[:, :units], 0.0))
    den_mean = links.sum_all(den_sum[None])[0] / (HEADS * seq_len * total_valid)

    def share_out(stacked):
        count = stacked.shape[0]
        by_slice = stacked.reshape(count, nb, 2, slice_dim, own)
        keep, got = (pick(by_slice, links.c, 2), links.core(pick(by_slice, links.c ^ 1, 2)))
        both = jnp.where(
            links.c == 0,
            jnp.concatenate([keep, got], axis=-1),
            jnp.concatenate([got, keep], axis=-1),
        )
        parts = [pick(both, links.b ^ d, 1) for d in range(nb)]
        parts = [links.across(p, d) if d else p for d, p in enumerate(parts)]
        plane = join_lanes(parts, [links.b ^ d for d in range(nb)])
        chain = [plane]
        for _ in range(nz - 1):
            chain.append(links.ring(chain[-1]))
        return join_lanes(chain, [links.behind(k) for k in range(nz)])

    gate_up = share_out(jnp.stack([gate_weight.T, up_weight.T]))
    down_cols = share_out(down_weight[None])[0]
    gate_cols, up_cols = (gate_up[0], gate_up[1])

    cot = by_plane(cotangent).reshape(tokens, width)
    cot_all = links.gather_plane(cot)

    resid_mid = inputs.reshape(tokens, width) + nt(y_low, w_out)
    n2_low = rms_norm(resid_mid, gain_mlp).astype(bf16)
    n2_all = links.gather_plane(n2_low)
    gate_act, up_act = (nt(n2_all, gate_cols), nt(n2_all, up_cols))
    sigma = jax.nn.sigmoid(gate_act)
    hidden_act = (gate_act * sigma * up_act).astype(bf16)
    d_hid = nt(cot_all, down_cols)
    d_gate = (d_hid * up_act * sigma * (1.0 + gate_act * (1.0 - sigma))).astype(bf16)
    d_up = (d_hid * gate_act * sigma).astype(bf16)
    back = (nn(d_gate, gate_cols) + nn(d_up, up_cols)).astype(bf16)
    d_n2 = links.scatter_plane(back.reshape(2, nb, tokens, width))
    down_part = nn(hidden_act, down_cols).astype(bf16)
    down_sum = links.scatter_plane(down_part.reshape(2, nb, tokens, width))
    hidden_out = by_owner((resid_mid + down_sum).astype(bf16)).reshape(rows, local, width)

    def give_back(*pairs):
        grads = [weight_grad(links, left, right) for left, right in pairs]
        sums = [
            links.scatter_ring([g[j] for j in range(nz)]).astype(bf16) for g in grads
        ]
        stacked = jnp.stack(sums).reshape(len(pairs), slice_dim, nb, 2 * own)
        stacked = jnp.moveaxis(stacked, 2, 0)
        parts = [pick(stacked, links.b ^ d) for d in range(nb)]
        parts = [links.across(p, d) if d else p for d, p in enumerate(parts)]
        mine = join_lead(parts, [links.b ^ d for d in range(nb)])
        mine = mine.reshape(nb, len(pairs), slice_dim, 2, own)
        keep, got = (pick(mine, links.c, 3), links.core(pick(mine, links.c ^ 1, 3)))
        both = jnp.where(links.c == 0, jnp.stack([keep, got], 1), jnp.stack([got, keep], 1))
        both = jnp.moveaxis(both, 2, 0).reshape(len(pairs), hidden_dim, own)
        return [both[i].astype(f32) for i in range(len(pairs))]

    (grad_down,) = give_back((hidden_act, cot_all))
    grad_gate, grad_up = (g.T for g in give_back((d_gate, n2_all), (d_up, n2_all)))

    _, norm_pull = jax.vjp(rms_norm, resid_mid, gain_mlp)
    d_mid_norm, grad_gain_mlp = norm_pull(d_n2)
    d_mid = cot.astype(f32) + d_mid_norm
    d_attn = d_mid.astype(bf16)
    d_y = nn(d_attn, w_out).astype(bf16).reshape(rows, local, groups, units * value_dim)
    d_pieces, _ = links.exchange_seq(d_y.swapaxes(1, 2).reshape(ns, local, units * value_dim))
    d_units = attend_back(
        pieces, sources, row_length[None], d_pieces, attn_units, den_units, units, block
    )
    back_pieces, back_sources = links.exchange_seq(d_units.reshape(ns, local, LANES * (units + 1)))
    d_all = join_lead(back_pieces, back_sources).reshape(rows, groups, local, -1).swapaxes(1, 2)
    d_proj = jnp.concatenate(
        [
            d_all[..., :LANES].reshape(tokens, qk_width),
            d_all[..., LANES:].reshape(tokens, width),
        ],
        axis=1,
    )

    def by_device(v):
        return v.reshape((nz, nb, 2, own) + v.shape[1:])

    grad_out = links.scatter_all(by_device(tn(d_attn, y_low).astype(bf16))).T
    packed_grad = links.scatter_all(by_device(tn(c_low, d_proj).astype(bf16)))
    grad_v = packed_grad[:, qk_width:]
    grad_qk = packed_grad[:, :qk_width].reshape(own, groups, 2, HALF)[..., : units * FEAT]
    grad_q = grad_qk[:, :, 0].reshape(own, HEADS * FEAT)
    grad_k = grad_qk[:, :, 1].reshape(own, HEADS * FEAT)

    d_c = nt(d_proj, w_in).reshape(rows, local, width)
    next_edge = lax.ppermute(
        d_c[:, :lag].astype(bf16), "seq", [(s + 1, s) for s in range(ns - 1)]
    ).astype(f32)
    d_extended = jnp.concatenate([d_c, next_edge], axis=1)
    d_n1 = sum(taps[j] * d_extended[:, j : j + local] for j in range(KERNEL))
    conv_rows = [
        jnp.sum(d_c * extended[:, lag - j : lag - j + local], axis=(0, 1)) for j in range(KERNEL)
    ]
    _, first_pull = jax.vjp(rms_norm, inputs, gain_attn)
    d_inputs, grad_gain_attn = first_pull(d_n1)
    hidden_grad = by_owner(d_mid.reshape(rows, local, width) + d_inputs)
    small_grads = jnp.stack([grad_gain_attn, grad_gain_mlp] + conv_rows)
    small_grads = jnp.moveaxis(small_grads.reshape(2 + KERNEL, nz, nb, 2, own), 0, 3)
    small_sum = links.scatter_all(small_grads)
    return (
        hidden_out,
        hidden_grad,
        grad_q,
        grad_k,
        grad_v,
        grad_out,
        small_sum[2:].T,
        small_sum[0],
        grad_gate,
        grad_up,
        grad_down,
        small_sum[1],
        den_mean,
    )


def solution(mesh):
    both = ("batch", "seq")
    tokens = P("batch", "seq", None)
    by_row, by_col, vector = (P(both, None), P(None, both), P(both))
    return jax.shard_map(
        on_device,
        mesh=mesh,
        in_specs=(
            tokens,
            P(),
            by_row,
            by_row,
            by_row,
            by_col,
            by_row,
            vector,
            by_row,
            by_row,
            by_col,
            vector,
            tokens,
        ),
        out_specs=(
            tokens,
            tokens,
            by_row,
            by_row,
            by_row,
            by_col,
            by_row,
            vector,
            by_row,
            by_row,
            by_col,
            vector,
            P(),
        ),
        check_vma=False,
    )
```

time: 2290 us -> 1120 us (0.49)
  waiting for transfers between devices: 1490 us -> 486 us
  blocking collectives: 289 us -> 0 us
  matrix products: 221 us -> 104 us
  starting transfers between devices: 17.1 us -> 131 us
  Pallas kernels: 0 us -> 89.9 us
  local copies, waits for them, and re-layouts: 174 us -> 203 us
    reduce_scatter x9 -> x0, waiting for transfers between devices: 784 us -> none  [the longest x1 186 us: on_device(): lax.psum_scatter(grad_v_full, ('batch', 'seq'), scatter_dimension=0, tile...]
    all_gather x11 -> x0, waiting for transfers between devices: 626 us -> none  [the longest x1 283 us: carried_in(): gathered = jax.tree.map(lambda a: lax.all_gather(a, axis), part)]
    ppermute x2 -> x155, waiting for transfers between devices: 1.84 us -> 486 us  [the longest x54 203 us: across(): return lax.ppermute(value, 'batch', [(b, b ^ d) for b in range(self.nb)])]
    ppermute x2 -> x155, starting transfers between devices: 2.76 us -> 131 us  [the longest x54 67.4 us: across(): return lax.ppermute(value, 'batch', [(b, b ^ d) for b in range(self.nb)])]
    all_to_all x3 -> x0, blocking collectives: 127 us -> none  [the longest x1 46.9 us: on_device(): lax.all_to_all(gate_weight, 'seq', split_axis=1, concat_axis=0, tiled=True)]
    dot_general x35 -> x12, matrix products: 221 us -> 104 us  [contract(): lax.dot_general(left, right, ((dims[:1], dims[1:]), ((), ())), preferred_...]
    pallas_call x0 -> x15, Pallas kernels: none -> 89.9 us  [the longest x3 32.9 us: weight_grad(): pl.pallas_call(kernel, out_shape=jax.ShapeDtypeStruct((links.nz, width, b...]
    all_gather x3 -> x0, blocking collectives: 80.9 us -> none  [the longest x1 41.2 us: on_device(): lax.all_gather(conv_weight, ('batch', 'seq'), axis=0, tiled=True)]
  transfers between devices with their start and end apart: 26 -> 155, of which waited for: 20 -> 65; matrix products, arithmetic and copies ran while one was open for 16% -> 34% of each run, Pallas kernels for 0% -> 6%
where the time goes in v1:
time: 1120 us; the launch traced here: 1110 us
  waiting for transfers between devices  486 us (43%)
  local copies, waits for them, and re-layouts  203 us (18%)
  starting transfers between devices  131 us (12%)
  matrix products  104 us (9%)
  Pallas kernels  89.9 us (8%)
  other arithmetic  89.3 us (8%)
    ppermute x54, waiting for transfers between devices, across(): return lax.ppermute(value, 'batch', [(b, b ^ d) for b in range(self.nb)])  203 us
    ppermute x36, waiting for transfers between devices, ring(): lax.ppermute(value, 'seq', [(s, (s + 2) % self.ns) for s in range(self.ns)])  199 us
    dot_general x12, matrix products, contract(): lax.dot_general(left, right, ((dims[:1], dims[1:]), ((), ())), preferred_...  104 us
    ppermute x28, waiting for transfers between devices, to_seq(): lax.ppermute(value, 'seq', [(s, 2 * ((s // 2 + dz) % self.nz) + (s % 2 ^...  82.7 us
    ppermute x54, starting transfers between devices, across(): return lax.ppermute(value, 'batch', [(b, b ^ d) for b in range(self.nb)])  67.4 us
    unnamed x228, local copies, waits for them, and re-layouts  43.9 us
    dynamic_slice x18, local copies, waits for them, and re-layouts, pick(): return lax.dynamic_index_in_dim(value, at, axis, False)  34.1 us
    pallas_call x3, Pallas kernels, weight_grad(): pl.pallas_call(kernel, out_shape=jax.ShapeDtypeStruct((links.nz, width, b...  32.9 us
  transfers between devices with their start and end apart: 155, of which 65 were waited for; matrix products, arithmetic and copies ran while one was open for 34% of the time, Pallas kernels for 6%

profile of v1, /device:TPU:0, one launch (start us, length us, event | category | flops | bytes accessed | tf_op | source)
XLA Modules:
  0.0 1113.0 jit_solution(12842470275372913954)
XLA Ops:
  76.2 11.8 %collective-permute-done.14 = bf16[64,2560]{1,0:T(8,128)(2,1)S(1)} collective-permute-done((bf16[64,2560]{1,0:T(8,128)(2,1)}, bf16[64,2560]{1,0:T(8,128)(2,1)S(1)}, u32[]{:S(2)}, u32[]{:S(2)}) %collective-permute-start.14) | collective-permute-done | bytes 327712 | tf_op jit(solution)/shard_map/ppermute | solution.py:61
  108.9 12.8 %collective-permute-done.69.refs_2_ = bf16[1,688,128]{2,1,0:T(8,128)(2,1)S(1)} collective-permute-done((bf16[1,688,128]{2,1,0:T(8,128)(2,1)}, bf16[1,688,128]{2,1,0:T(8,128)(2,1)S(1)}, u32[]{:S(2)}, u32[]{:S(2)}) %collective-permute-start.69) | collective-permute-done | bytes 176160 | tf_op jit(solution)/shard_map/ppermute | solution.py:64
  124.2 7.5 collective-permute-done.70.refs_3_
  148.7 19.5 %collective-permute-done.61.refs_1_ = bf16[2,688,128]{2,1,0:T(8,128)(2,1)S(1)} collective-permute-done((bf16[2,688,128]{2,1,0:T(8,128)(2,1)}, bf16[2,688,128]{2,1,0:T(8,128)(2,1)S(1)}, u32[]{:S(2)}, u32[]{:S(2)}) %collective-permute-start.61) | collective-permute-done | bytes 352288 | tf_op jit(solution)/shard_map/ppermute | solution.py:64
  181.1 29.1 %collective-permute-done.81 = bf16[128,2048]{1,0:T(8,128)(2,1)} collective-permute-done((bf16[128,2048]{1,0:T(8,128)(2,1)S(1)}, bf16[128,2048]{1,0:T(8,128)(2,1)}, u32[]{:S(2)}, u32[]{:S(2)}) %collective-permute-start.81) | collective-permute-done | bytes 524320 | tf_op jit(solution)/shard_map/ppermute | solution.py:64
  214.0 13.1 %collective-permute-done.18.refs_3_ = bf16[2,64,2560]{2,1,0:T(8,128)(2,1)} collective-permute-done((bf16[2,64,2560]{2,1,0:T(8,128)(2,1)}, bf16[2,64,2560]{2,1,0:T(8,128)(2,1)}, u32[]{:S(2)}, u32[]{:S(2)}) %collective-permute-start.18) | collective-permute-done | bytes 655392 | tf_op jit(solution)/shard_map/ppermute | solution.py:64
  250.0 8.6 shard_map.228
  278.3 16.4 %collective-permute-done.64.refs_1_ = bf16[2,688,512]{2,1,0:T(8,128)(2,1)} collective-permute-done((bf16[2,688,512]{2,1,0:T(8,128)(2,1)S(1)}, bf16[2,688,512]{2,1,0:T(8,128)(2,1)}, u32[]{:S(2)}, u32[]{:S(2)}) %collective-permute-start.64) | collective-permute-done | bytes 1409056 | tf_op jit(solution)/shard_map/ppermute | solution.py:61
  300.6 9.5 collective-permute-done.73.refs_3_
  310.0 32.8 %collective-permute-done.31.refs_7_ = bf16[128,640]{1,0:T(8,128)(2,1)S(1)} collective-permute-done((bf16[128,640]{1,0:T(8,128)(2,1)S(1)}, bf16[128,640]{1,0:T(8,128)(2,1)S(1)}, u32[]{:S(2)}, u32[]{:S(2)}) %collective-permute-start.31) | collective-permute-done | bytes 163872 | tf_op jit(solution)/shard_map/ppermute | solution.py:67
  349.2 7.8 collective-permute-done.29.refs_5_
  371.6 6.6 shard_map.229
  391.4 6.5 shard_map.231
  415.8 10.8 fusion.2
  426.7 11.8 %collective-permute-done.52 = bf16[256,2048]{1,0:T(8,128)(2,1)S(1)} collective-permute-done((bf16[256,2048]{1,0:T(8,128)(2,1)S(1)}, bf16[256,2048]{1,0:T(8,128)(2,1)S(1)}, u32[]{:S(2)}, u32[]{:S(2)}) %collective-permute-start.52) | collective-permute-done | bytes 1048608 | tf_op jit(solution)/shard_map/ppermute | solution.py:64
  444.4 6.1 collective-permute-start.150
  470.9 10.9 fusion.9
  481.8 16.4 %multiply_convert_fusion.1 = (bf16[2048,688]{1,0:T(8,128)(2,1)}, bf16[2048,688]{1,0:T(8,128)(2,1)}, bf16[2048,688]{1,0:T(8,128)(2,1)}) fusion(f32[2048,688]{1,0:T(8,128)} %fusion.2, f32[2048,688]{1,0:T(8,128)} %fusion.9, bf16[2048,2048]{1,0:T(8,128)(2,1)} %constant_dynamic-update-slice_fusion.2.right_ref, bf16[2,688,2048]{2,1,0:T(8,128)(2,1)S(1)} %shard_map.233), kind=kOutput, calls=%fused_computation.11 | convolution fusion | flops 5793906688 | bytes 30932992 | tf_op jit(solution)/shard_map/dot_general | solution.py:29
  498.2 11.0 shard_map.241
  509.1 11.2 %convolution_convert_fusion.2 = bf16[2048,2048]{1,0:T(8,128)(2,1)} fusion(bf16[2048,688]{1,0:T(8,128)(2,1)} %get-tuple-element.37.left_ref, bf16[1,688,2048]{2,1,0:T(8,128)(2,1)} %copy-done.2), kind=kOutput, calls=%fused_computation.9 | convolution fusion | flops 5775556608 | bytes 14024704 | tf_op jit(solution)/shard_map/dot_general | solution.py:29
  520.3 11.0 shard_map.239
  531.3 12.4 %fusion.8 = f32[2048,2048]{1,0:T(8,128)} fusion(bf16[2048,688]{1,0:T(8,128)(2,1)} %get-tuple-element.38.left_ref, bf16[2,688,2048]{2,1,0:T(8,128)(2,1)S(1)} %shard_map.233), kind=kOutput, calls=%fused_computation.31 | convolution fusion | flops 5771362304 | bytes 22413312 | tf_op jit(solution)/shard_map/dot_general | solution.py:29
  547.4 10.9 shard_map.238
  558.4 13.2 %add_convert_fusion = bf16[2048,2048]{1,0:T(8,128)(2,1)} fusion(f32[2048,2048]{1,0:T(8,128)} %fusion.8, bf16[2048,688]{1,0:T(8,128)(2,1)} %get-tuple-element.36.left_ref, bf16[2,688,2048]{2,1,0:T(8,128)(2,1)S(1)} %shard_map.233), kind=kOutput, calls=%fused_computation | convolution fusion | flops 5779750912 | bytes 30801920 | tf_op jit(solution)/shard_map/dot_general | solution.py:29
  571.6 7.0 fusion.64
  580.5 6.0 fusion.65
  586.8 12.4 %collective-permute-done.132 = bf16[688,512]{1,0:T(8,128)(2,1)S(1)} collective-permute-done((bf16[688,512]{1,0:T(8,128)(2,1)S(1)}, bf16[688,512]{1,0:T(8,128)(2,1)S(1)}, u32[]{:S(2)}, u32[]{:S(2)}) %collective-permute-start.132) | collective-permute-done | bytes 704544 | tf_op jit(solution)/shard_map/ppermute | solution.py:61
  599.4 14.8 %collective-permute-done.135 = bf16[688,512]{1,0:T(8,128)(2,1)S(1)} collective-permute-done((bf16[688,512]{1,0:T(8,128)(2,1)S(1)}, bf16[688,512]{1,0:T(8,128)(2,1)S(1)}, u32[]{:S(2)}, u32[]{:S(2)}) %collective-permute-start.135) | collective-permute-done | bytes 704544 | tf_op jit(solution)/shard_map/ppermute | solution.py:61
  614.4 14.9 %collective-permute-done.143 = bf16[688,512]{1,0:T(8,128)(2,1)S(1)} collective-permute-done((bf16[688,512]{1,0:T(8,128)(2,1)S(1)}, bf16[688,512]{1,0:T(8,128)(2,1)S(1)}, u32[]{:S(2)}, u32[]{:S(2)}) %collective-permute-start.143) | collective-permute-done | bytes 704544 | tf_op jit(solution)/shard_map/ppermute | solution.py:61
  629.5 14.9 %collective-permute-done.133 = bf16[688,512]{1,0:T(8,128)(2,1)S(1)} collective-permute-done((bf16[688,512]{1,0:T(8,128)(2,1)S(1)}, bf16[688,512]{1,0:T(8,128)(2,1)S(1)}, u32[]{:S(2)}, u32[]{:S(2)}) %collective-permute-start.133) | collective-permute-done | bytes 704544 | tf_op jit(solution)/shard_map/ppermute | solution.py:61
  645.8 13.7 %collective-permute-done.136 = bf16[688,512]{1,0:T(8,128)(2,1)S(1)} collective-permute-done((bf16[688,512]{1,0:T(8,128)(2,1)S(1)}, bf16[688,512]{1,0:T(8,128)(2,1)S(1)}, u32[]{:S(2)}, u32[]{:S(2)}) %collective-permute-start.136) | collective-permute-done | bytes 704544 | tf_op jit(solution)/shard_map/ppermute | solution.py:61
  660.6 14.0 %collective-permute-done.144 = bf16[688,512]{1,0:T(8,128)(2,1)S(1)} collective-permute-done((bf16[688,512]{1,0:T(8,128)(2,1)S(1)}, bf16[688,512]{1,0:T(8,128)(2,1)S(1)}, u32[]{:S(2)}, u32[]{:S(2)}) %collective-permute-start.144) | collective-permute-done | bytes 704544 | tf_op jit(solution)/shard_map/ppermute | solution.py:61
  675.1 14.7 %collective-permute-done.134 = bf16[688,512]{1,0:T(8,128)(2,1)} collective-permute-done((bf16[688,512]{1,0:T(8,128)(2,1)S(1)}, bf16[688,512]{1,0:T(8,128)(2,1)}, u32[]{:S(2)}, u32[]{:S(2)}) %collective-permute-start.134) | collective-permute-done | bytes 704544 | tf_op jit(solution)/shard_map/ppermute | solution.py:61
  692.4 12.1 %collective-permute-done.137 = bf16[688,512]{1,0:T(8,128)(2,1)} collective-permute-done((bf16[688,512]{1,0:T(8,128)(2,1)}, bf16[688,512]{1,0:T(8,128)(2,1)}, u32[]{:S(2)}, u32[]{:S(2)}) %collective-permute-start.137) | collective-permute-done | bytes 704544 | tf_op jit(solution)/shard_map/ppermute | solution.py:61
  706.9 8.0 convert_add_fusion.2
  721.7 8.9 fusion.61
  740.1 7.1 collective-permute-done.77
  761.5 9.1 collective-permute-done.92
  775.8 17.4 %collective-permute-done.78 = bf16[256,2048]{1,0:T(8,128)(2,1)} collective-permute-done((bf16[256,2048]{1,0:T(8,128)(2,1)}, bf16[256,2048]{1,0:T(8,128)(2,1)}, u32[]{:S(2)}, u32[]{:S(2)}) %collective-permute-start.78) | collective-permute-done | bytes 1048608 | tf_op jit(solution)/shard_map/ppermute | solution.py:64
  796.2 6.0 fusion.14
  829.6 10.5 collective-permute-done.97.refs_13_
  844.1 21.6 %shard_map.236 = bf16[1024,640]{1,0:T(8,128)(2,1)} custom-call(s32[8]{0:T(128)} %copy-done.14, s32[1]{0:T(128)} %dynamic_slice.269.length_ref, bf16[128,640]{1,0:T(8,128)(2,1)} %copy-done.12, bf16[128,640]{1,0:T(8,128)(2,1)} %copy-done.22, bf16[128,640]{1,0:T(8,128)(2,1)} %copy-done.21, bf16[128,640]{1,0:T(8,128)(2,1)} %copy-done.20, ...), custom_call_target="tpu_custom_call" | custom-call | flops 5033164800 | bytes 8388608 | tf_op jit(solution)/shard_map/pallas_call | solution.py:421
  907.8 9.0 constant_dynamic-slice_fusion.20
  1006.8 6.4 collective-permute-done.117
  1016.7 10.5 collective-permute-done.109
  1031.9 17.8 %collective-permute-done.120 = bf16[4,64,2048]{2,1,0:T(8,128)(2,1)S(1)} collective-permute-done((bf16[4,64,2048]{2,1,0:T(8,128)(2,1)S(1)}, bf16[4,64,2048]{2,1,0:T(8,128)(2,1)S(1)}, u32[]{:S(2)}, u32[]{:S(2)}) %collective-permute-start.120) | collective-permute-done | bytes 1048608 | tf_op jit(solution)/shard_map/ppermute | solution.py:64
  1052.7 20.9 %collective-permute-done.112 = bf16[4,64,2560]{2,1,0:T(8,128)(2,1)S(1)} collective-permute-done((bf16[4,64,2560]{2,1,0:T(8,128)(2,1)S(1)}, bf16[4,64,2560]{2,1,0:T(8,128)(2,1)S(1)}, u32[]{:S(2)}, u32[]{:S(2)}) %collective-permute-start.112) | collective-permute-done | bytes 1310752 | tf_op jit(solution)/shard_map/ppermute | solution.py:64
  1078.9 7.5 collective-permute-done.113
  (748 shorter events, 510.9 us)
Async XLA Ops:
  1.4 47.5 %collective-permute-start = (bf16[5,64]{1,0:T(8,128)(2,1)S(1)}, bf16[5,64]{1,0:T(8,128)(2,1)S(1)}, u32[]{:S(2)}, u32[]{:S(2)}) collective-permute-start(bf16[5,64]{1,0:T(8,128)(2,1)S(1)} %get-tuple-element.153), channel_id=1, source_target_pairs={{0,2},{1,3},{2,4},{3,5},{4,6},{5,7},{6,0},{7,1},{8,10},{9,11},{10,... | collective-permute-start | bytes 1928 | tf_op jit(solution)/shard_map/ppermute | solution.py:61
  4.4 91.3 %collective-permute-start.39 = (bf16[64,2048]{1,0:T(8,128)(2,1)}, bf16[64,2048]{1,0:T(8,128)(2,1)}, u32[]{:S(2)}, u32[]{:S(2)}) collective-permute-start(bf16[64,2048]{1,0:T(8,128)(2,1)} %bitcast.577), channel_id=1, source_target_pairs={{0,2},{1,3},{2,4},{3,5},{4,6},{5,7},{6,0},{7,1},{8,10},{9,11},{10,... | collective-permute-start | bytes 786440 | tf_op jit(solution)/shard_map/ppermute | solution.py:61
  8.8 67.3 %collective-permute-start.13 = (bf16[64,2560]{1,0:T(8,128)(2,1)S(1)}, bf16[64,2560]{1,0:T(8,128)(2,1)}, u32[]{:S(2)}, u32[]{:S(2)}) collective-permute-start(bf16[64,2560]{1,0:T(8,128)(2,1)S(1)} %constant_dynamic-update-slice_fusion), channel_id=1, source_target_pairs={{0,2},{1,3},{2,4},{3,5},{4,6},{5,7},{6,0},{7,1},{8,10},{9,11},{10,... | collective-permute-start | bytes 983048 | tf_op jit(solution)/shard_map/ppermute | solution.py:61
  17.3 70.7 %collective-permute-start.67 = (bf16[1,4,688,64]{2,3,1,0:T(8,128)(2,1)}, bf16[1,4,688,64]{2,3,1,0:T(8,128)(2,1)}, u32[]{:S(2)}, u32[]{:S(2)}) collective-permute-start(bf16[1,4,688,64]{2,3,1,0:T(8,128)(2,1)} %bitcast.523), channel_id=1, source_target_pairs={{0,1},{1,0},{2,3},{3,2},{4,5},{5,4},{6,7},{7,6},{8,9},{9,8},{10,11... | collective-permute-start | bytes 1056776 | tf_op jit(solution)/shard_map/ppermute | solution.py:58
  91.8 50.5 %collective-permute-start.80 = (bf16[256,2048]{1,0:T(8,128)(2,1)}, bf16[256,2048]{1,0:T(8,128)(2,1)}, u32[]{:S(2)}, u32[]{:S(2)}) collective-permute-start(bf16[256,2048]{1,0:T(8,128)(2,1)} %reshape_reshape.7), channel_id=1, source_target_pairs={{0,16},{8,24},{16,0},{24,8},{1,17},{9,25},{17,1},{25,9},{2,18},{10... | collective-permute-start | bytes 3145736 | tf_op jit(solution)/shard_map/ppermute | solution.py:64
  93.3 39.5 %collective-permute-start.60 = (bf16[2,4,688,64]{2,3,1,0:T(8,128)(2,1)}, bf16[2,4,688,64]{2,3,1,0:T(8,128)(2,1)}, u32[]{:S(2)}, u32[]{:S(2)}) collective-permute-start(bf16[2,4,688,64]{2,3,1,0:T(8,128)(2,1)} %get-tuple-element.86), channel_id=1, source_target_pairs={{0,1},{1,0},{2,3},{3,2},{4,5},{5,4},{6,7},{7,6},{8,9},{9,8},{10,11... | collective-permute-start | bytes 2113544 | tf_op jit(solution)/shard_map/ppermute | solution.py:58
  101.6 44.6 %collective-permute-start.79 = (bf16[256,2048]{1,0:T(8,128)(2,1)}, bf16[256,2048]{1,0:T(8,128)(2,1)}, u32[]{:S(2)}, u32[]{:S(2)}) collective-permute-start(bf16[256,2048]{1,0:T(8,128)(2,1)} %reshape_reshape.7), channel_id=1, source_target_pairs={{0,8},{8,0},{16,24},{24,16},{1,9},{9,1},{17,25},{25,17},{2,10},{10... | collective-permute-start | bytes 3145736 | tf_op jit(solution)/shard_map/ppermute | solution.py:64
  107.2 62.7 %collective-permute-start.17 = (bf16[4,64,2560]{2,1,0:T(8,128)(2,1)S(1)}, bf16[4,64,2560]{2,1,0:T(8,128)(2,1)}, u32[]{:S(2)}, u32[]{:S(2)}) collective-permute-start(bf16[4,64,2560]{2,1,0:T(8,128)(2,1)S(1)} %pad_maximum_fusion.2.refs_0_), channel_id=1, source_target_pairs={{0,16},{8,24},{16,0},{24,8},{1,17},{9,25},{17,1},{25,9},{2,18},{10... | collective-permute-start | bytes 3932168 | tf_op jit(solution)/shard_map/ppermute | solution.py:64
  131.7 45.5 %collective-permute-start.16 = (bf16[4,64,2560]{2,1,0:T(8,128)(2,1)S(1)}, bf16[4,64,2560]{2,1,0:T(8,128)(2,1)}, u32[]{:S(2)}, u32[]{:S(2)}) collective-permute-start(bf16[4,64,2560]{2,1,0:T(8,128)(2,1)S(1)} %pad_maximum_fusion.2.refs_0_), channel_id=1, source_target_pairs={{0,8},{8,0},{16,24},{24,16},{1,9},{9,1},{17,25},{25,17},{2,10},{10... | collective-permute-start | bytes 3932168 | tf_op jit(solution)/shard_map/ppermute | solution.py:64
  146.2 34.9 %collective-permute-start.71 = (bf16[1,688,512]{2,1,0:T(8,128)(2,1)S(1)}, bf16[1,688,512]{2,1,0:T(8,128)(2,1)}, u32[]{:S(2)}, u32[]{:S(2)}) collective-permute-start(bf16[1,688,512]{2,1,0:T(8,128)(2,1)S(1)} %shard_map.234.refs_0_), channel_id=1, source_target_pairs={{0,2},{1,3},{2,4},{3,5},{4,6},{5,7},{6,0},{7,1},{8,10},{9,11},{10,... | collective-permute-start | bytes 2113544 | tf_op jit(solution)/shard_map/ppermute | solution.py:61
  169.8 41.4 %collective-permute-start.43 = (bf16[4,64,2048]{2,1,0:T(8,128)(2,1)S(1)}, bf16[4,64,2048]{2,1,0:T(8,128)(2,1)}, u32[]{:S(2)}, u32[]{:S(2)}) collective-permute-start(bf16[4,64,2048]{2,1,0:T(8,128)(2,1)S(1)} %pad_maximum_fusion.5.refs_0_), channel_id=1, source_target_pairs={{0,16},{8,24},{16,0},{24,8},{1,17},{9,25},{17,1},{25,9},{2,18},{10... | collective-permute-start | bytes 3145736 | tf_op jit(solution)/shard_map/ppermute | solution.py:64
  170.0 40.3 %collective-permute-start.81 = (bf16[128,2048]{1,0:T(8,128)(2,1)S(1)}, bf16[128,2048]{1,0:T(8,128)(2,1)}, u32[]{:S(2)}, u32[]{:S(2)}) collective-permute-start(bf16[128,2048]{1,0:T(8,128)(2,1)S(1)} %slice.625), channel_id=1, source_target_pairs={{0,16},{8,24},{16,0},{24,8},{1,17},{9,25},{17,1},{25,9},{2,18},{10... | collective-permute-start | bytes 1572872 | tf_op jit(solution)/shard_map/ppermute | solution.py:64
  177.1 36.7 %collective-permute-start.42 = (bf16[4,64,2048]{2,1,0:T(8,128)(2,1)S(1)}, bf16[4,64,2048]{2,1,0:T(8,128)(2,1)}, u32[]{:S(2)}, u32[]{:S(2)}) collective-permute-start(bf16[4,64,2048]{2,1,0:T(8,128)(2,1)S(1)} %pad_maximum_fusion.5.refs_0_), channel_id=1, source_target_pairs={{0,8},{8,0},{16,24},{24,16},{1,9},{9,1},{17,25},{25,17},{2,10},{10... | collective-permute-start | bytes 3145736 | tf_op jit(solution)/shard_map/ppermute | solution.py:64
  177.2 36.2 %collective-permute-start.19 = (bf16[2,64,2560]{2,1,0:T(8,128)(2,1)}, bf16[2,64,2560]{2,1,0:T(8,128)(2,1)}, u32[]{:S(2)}, u32[]{:S(2)}) collective-permute-start(bf16[2,64,2560]{2,1,0:T(8,128)(2,1)} %slice.606), channel_id=1, source_target_pairs={{0,8},{8,0},{16,24},{24,16},{1,9},{9,1},{17,25},{25,17},{2,10},{10... | collective-permute-start | bytes 1966088 | tf_op jit(solution)/shard_map/ppermute | solution.py:64
  181.1 46.4 %collective-permute-start.20 = (bf16[4,64,2560]{2,1,0:T(8,128)(2,1)S(1)}, bf16[4,64,2560]{2,1,0:T(8,128)(2,1)}, u32[]{:S(2)}, u32[]{:S(2)}) collective-permute-start(bf16[4,64,2560]{2,1,0:T(8,128)(2,1)S(1)} %pad_maximum_fusion.2.refs_0_), channel_id=1, source_target_pairs={{0,1},{1,0},{2,3},{3,2},{4,5},{5,4},{6,7},{7,6},{8,9},{9,8},{10,11... | collective-permute-start | bytes 3932168 | tf_op jit(solution)/shard_map/ppermute | solution.py:58
  258.7 36.1 %collective-permute-start.84 = (bf16[256,2048]{1,0:T(8,128)(2,1)}, bf16[256,2048]{1,0:T(8,128)(2,1)}, u32[]{:S(2)}, u32[]{:S(2)}) collective-permute-start(bf16[256,2048]{1,0:T(8,128)(2,1)} %collective-permute-done.79), channel_id=1, source_target_pairs={{0,1},{1,0},{2,3},{3,2},{4,5},{5,4},{6,7},{7,6},{8,9},{9,8},{10,11... | collective-permute-start | bytes 3145736 | tf_op jit(solution)/shard_map/ppermute | solution.py:58
  259.1 35.6 %collective-permute-start.64 = (bf16[2,688,512]{2,1,0:T(8,128)(2,1)S(1)}, bf16[2,688,512]{2,1,0:T(8,128)(2,1)}, u32[]{:S(2)}, u32[]{:S(2)}) collective-permute-start(bf16[2,688,512]{2,1,0:T(8,128)(2,1)S(1)} %shard_map.232.refs_0_), channel_id=1, source_target_pairs={{0,2},{1,3},{2,4},{3,5},{4,6},{5,7},{6,0},{7,1},{8,10},{9,11},{10,... | collective-permute-start | bytes 4227080 | tf_op jit(solution)/shard_map/ppermute | solution.py:61
  272.5 37.5 %collective-permute-start.73 = (bf16[1,688,512]{2,1,0:T(8,128)(2,1)}, bf16[1,688,512]{2,1,0:T(8,128)(2,1)}, u32[]{:S(2)}, u32[]{:S(2)}) collective-permute-start(bf16[1,688,512]{2,1,0:T(8,128)(2,1)} %copy-done.3), channel_id=1, source_target_pairs={{0,2},{1,3},{2,4},{3,5},{4,6},{5,7},{6,0},{7,1},{8,10},{9,11},{10,... | collective-permute-start | bytes 2113544 | tf_op jit(solution)/shard_map/ppermute | solution.py:61
  294.7 89.1 %collective-permute-start.65 = (bf16[2,688,512]{2,1,0:T(8,128)(2,1)}, bf16[2,688,512]{2,1,0:T(8,128)(2,1)S(1)}, u32[]{:S(2)}, u32[]{:S(2)}) collective-permute-start(bf16[2,688,512]{2,1,0:T(8,128)(2,1)} %collective-permute-done.64.refs_1_), channel_id=1, source_target_pairs={{0,2},{1,3},{2,4},{3,5},{4,6},{5,7},{6,0},{7,1},{8,10},{9,11},{10,... | collective-permute-start | bytes 4227080 | tf_op jit(solution)/shard_map/ppermute | solution.py:61
  294.8 48.1 %collective-permute-start.31 = (bf16[128,640]{1,0:T(8,128)(2,1)S(1)}, bf16[128,640]{1,0:T(8,128)(2,1)S(1)}, u32[]{:S(2)}, u32[]{:S(2)}) collective-permute-start(bf16[128,640]{1,0:T(8,128)(2,1)S(1)} %get-tuple-element.99), channel_id=1, source_target_pairs={{0,7},{1,6},{2,1},{3,0},{4,3},{5,2},{6,5},{7,4},{8,15},{9,14},{10,... | collective-permute-start | bytes 491528 | tf_op jit(solution)/shard_map/ppermute | solution.py:67
  296.4 49.7 %collective-permute-start.30 = (bf16[128,640]{1,0:T(8,128)(2,1)S(1)}, bf16[128,640]{1,0:T(8,128)(2,1)S(1)}, u32[]{:S(2)}, u32[]{:S(2)}) collective-permute-start(bf16[128,640]{1,0:T(8,128)(2,1)S(1)} %get-tuple-element.100), channel_id=1, source_target_pairs={{0,6},{1,7},{2,0},{3,1},{4,2},{5,3},{6,4},{7,5},{8,14},{9,15},{10,... | collective-permute-start | bytes 491528 | tf_op jit(solution)/shard_map/ppermute | solution.py:67
  300.5 77.9 %collective-permute-start.48 = (bf16[4,64,2048]{2,1,0:T(8,128)(2,1)}, bf16[4,64,2048]{2,1,0:T(8,128)(2,1)S(1)}, u32[]{:S(2)}, u32[]{:S(2)}) collective-permute-start(bf16[4,64,2048]{2,1,0:T(8,128)(2,1)} %collective-permute-done.43.refs_2_), channel_id=1, source_target_pairs={{0,1},{1,0},{2,3},{3,2},{4,5},{5,4},{6,7},{7,6},{8,9},{9,8},{10,11... | collective-permute-start | bytes 3145736 | tf_op jit(solution)/shard_map/ppermute | solution.py:58
  310.0 73.2 %collective-permute-start.47 = (bf16[4,64,2048]{2,1,0:T(8,128)(2,1)}, bf16[4,64,2048]{2,1,0:T(8,128)(2,1)S(1)}, u32[]{:S(2)}, u32[]{:S(2)}) collective-permute-start(bf16[4,64,2048]{2,1,0:T(8,128)(2,1)} %collective-permute-done.42.refs_1_), channel_id=1, source_target_pairs={{0,1},{1,0},{2,3},{3,2},{4,5},{5,4},{6,7},{7,6},{8,9},{9,8},{10,11... | collective-permute-start | bytes 3145736 | tf_op jit(solution)/shard_map/ppermute | solution.py:58
  399.3 58.5 %collective-permute-start.66 = (bf16[2,688,512]{2,1,0:T(8,128)(2,1)S(1)}, bf16[2,688,512]{2,1,0:T(8,128)(2,1)S(1)}, u32[]{:S(2)}, u32[]{:S(2)}) collective-permute-start(bf16[2,688,512]{2,1,0:T(8,128)(2,1)S(1)} %collective-permute-done.65.refs_2_), channel_id=1, source_target_pairs={{0,2},{1,3},{2,4},{3,5},{4,6},{5,7},{6,0},{7,1},{8,10},{9,11},{10,... | collective-permute-start | bytes 4227080 | tf_op jit(solution)/shard_map/ppermute | solution.py:61
  426.6 38.8 %collective-permute-start.55 = (bf16[256,2048]{1,0:T(8,128)(2,1)S(1)}, bf16[256,2048]{1,0:T(8,128)(2,1)S(1)}, u32[]{:S(2)}, u32[]{:S(2)}) collective-permute-start(bf16[256,2048]{1,0:T(8,128)(2,1)S(1)} %get-tuple-element.35), channel_id=1, source_target_pairs={{0,1},{1,0},{2,3},{3,2},{4,5},{5,4},{6,7},{7,6},{8,9},{9,8},{10,11... | collective-permute-start | bytes 3145736 | tf_op jit(solution)/shard_map/ppermute | solution.py:58
  461.5 137.9 %collective-permute-start.152 = (f32[1]{0:T(128)}, f32[1]{0:T(128)}, u32[]{:S(2)}, u32[]{:S(2)}) collective-permute-start(f32[1]{0:T(128)} %add.1190), channel_id=1, source_target_pairs={{0,2},{1,3},{2,4},{3,5},{4,6},{5,7},{6,0},{7,1},{8,10},{9,11},{10,... | collective-permute-start | bytes 20 | tf_op jit(solution)/shard_map/ppermute | solution.py:61
  544.9 41.6 %collective-permute-start.142 = (bf16[688,512]{1,0:T(8,128)(2,1)S(1)}, bf16[688,512]{1,0:T(8,128)(2,1)S(1)}, u32[]{:S(2)}, u32[]{:S(2)}) collective-permute-start(bf16[688,512]{1,0:T(8,128)(2,1)S(1)} %slice_bitcast_fusion.15), channel_id=1, source_target_pairs={{0,2},{1,3},{2,4},{3,5},{4,6},{5,7},{6,0},{7,1},{8,10},{9,11},{10,... | collective-permute-start | bytes 2113544 | tf_op jit(solution)/shard_map/ppermute | solution.py:61
  578.6 128.3 %collective-permute-start.88 = (bf16[4,256,2048]{2,1,0:T(8,128)(2,1)}, bf16[4,256,2048]{2,1,0:T(8,128)(2,1)}, u32[]{:S(2)}, u32[]{:S(2)}) collective-permute-start(bf16[4,256,2048]{2,1,0:T(8,128)(2,1)} %bitcast.117), channel_id=1, source_target_pairs={{0,1},{1,0},{2,3},{3,2},{4,5},{5,4},{6,7},{7,6},{8,9},{9,8},{10,11... | collective-permute-start | bytes 12582920 | tf_op jit(solution)/shard_map/ppermute | solution.py:58
  579.5 34.7 %collective-permute-start.135 = (bf16[688,512]{1,0:T(8,128)(2,1)S(1)}, bf16[688,512]{1,0:T(8,128)(2,1)S(1)}, u32[]{:S(2)}, u32[]{:S(2)}) collective-permute-start(bf16[688,512]{1,0:T(8,128)(2,1)S(1)} %slice_bitcast_fusion.19), channel_id=1, source_target_pairs={{0,2},{1,3},{2,4},{3,5},{4,6},{5,7},{6,0},{7,1},{8,10},{9,11},{10,... | collective-permute-start | bytes 2113544 | tf_op jit(solution)/shard_map/ppermute | solution.py:61
  586.5 135.2 %collective-permute-start.74 = (bf16[4,256,2048]{2,1,0:T(8,128)(2,1)}, bf16[4,256,2048]{2,1,0:T(8,128)(2,1)}, u32[]{:S(2)}, u32[]{:S(2)}) collective-permute-start(bf16[4,256,2048]{2,1,0:T(8,128)(2,1)} %bitcast.106), channel_id=1, source_target_pairs={{0,1},{1,0},{2,3},{3,2},{4,5},{5,4},{6,7},{7,6},{8,9},{9,8},{10,11... | collective-permute-start | bytes 12582920 | tf_op jit(solution)/shard_map/ppermute | solution.py:58
  599.3 45.1 %collective-permute-start.133 = (bf16[688,512]{1,0:T(8,128)(2,1)S(1)}, bf16[688,512]{1,0:T(8,128)(2,1)S(1)}, u32[]{:S(2)}, u32[]{:S(2)}) collective-permute-start(bf16[688,512]{1,0:T(8,128)(2,1)S(1)} %fusion.34), channel_id=1, source_target_pairs={{0,2},{1,3},{2,4},{3,5},{4,6},{5,7},{6,0},{7,1},{8,10},{9,11},{10,... | collective-permute-start | bytes 2113544 | tf_op jit(solution)/shard_map/ppermute | solution.py:61
  644.6 45.2 %collective-permute-start.134 = (bf16[688,512]{1,0:T(8,128)(2,1)S(1)}, bf16[688,512]{1,0:T(8,128)(2,1)}, u32[]{:S(2)}, u32[]{:S(2)}) collective-permute-start(bf16[688,512]{1,0:T(8,128)(2,1)S(1)} %fusion.33), channel_id=1, source_target_pairs={{0,2},{1,3},{2,4},{3,5},{4,6},{5,7},{6,0},{7,1},{8,10},{9,11},{10,... | collective-permute-start | bytes 2113544 | tf_op jit(solution)/shard_map/ppermute | solution.py:61
  659.5 149.6 %collective-permute-start.154 = (f32[1]{0:T(128)}, f32[1]{0:T(128)}, u32[]{:S(2)}, u32[]{:S(2)}) collective-permute-start(f32[1]{0:T(128)} %collective-permute-done.153), channel_id=1, source_target_pairs={{0,2},{1,3},{2,4},{3,5},{4,6},{5,7},{6,0},{7,1},{8,10},{9,11},{10,... | collective-permute-start | bytes 20 | tf_op jit(solution)/shard_map/ppermute | solution.py:61
  736.9 33.7 %collective-permute-start.92 = (bf16[256,2048]{1,0:T(8,128)(2,1)}, bf16[256,2048]{1,0:T(8,128)(2,1)S(1)}, u32[]{:S(2)}, u32[]{:S(2)}) collective-permute-start(bf16[256,2048]{1,0:T(8,128)(2,1)} %pad_maximum_fusion.9), channel_id=1, source_target_pairs={{0,16},{8,24},{16,0},{24,8},{1,17},{9,25},{17,1},{25,9},{2,18},{10... | collective-permute-start | bytes 3145736 | tf_op jit(solution)/shard_map/ppermute | solution.py:64
  739.0 32.7 %collective-permute-start.90 = (bf16[256,2048]{1,0:T(8,128)(2,1)}, bf16[256,2048]{1,0:T(8,128)(2,1)}, u32[]{:S(2)}, u32[]{:S(2)}) collective-permute-start(bf16[256,2048]{1,0:T(8,128)(2,1)} %pad_maximum_fusion.8), channel_id=1, source_target_pairs={{0,8},{8,0},{16,24},{24,16},{1,9},{9,1},{17,25},{25,17},{2,10},{10... | collective-permute-start | bytes 3145736 | tf_op jit(solution)/shard_map/ppermute | solution.py:64
  751.1 42.2 %collective-permute-start.78 = (bf16[256,2048]{1,0:T(8,128)(2,1)}, bf16[256,2048]{1,0:T(8,128)(2,1)}, u32[]{:S(2)}, u32[]{:S(2)}) collective-permute-start(bf16[256,2048]{1,0:T(8,128)(2,1)} %pad_maximum_fusion.7), channel_id=1, source_target_pairs={{0,16},{8,24},{16,0},{24,8},{1,17},{9,25},{17,1},{25,9},{2,18},{10... | collective-permute-start | bytes 3145736 | tf_op jit(solution)/shard_map/ppermute | solution.py:64
  752.9 41.8 %collective-permute-start.76 = (bf16[256,2048]{1,0:T(8,128)(2,1)}, bf16[256,2048]{1,0:T(8,128)(2,1)}, u32[]{:S(2)}, u32[]{:S(2)}) collective-permute-start(bf16[256,2048]{1,0:T(8,128)(2,1)} %pad_maximum_fusion.6), channel_id=1, source_target_pairs={{0,8},{8,0},{16,24},{24,16},{1,9},{9,1},{17,25},{25,17},{2,10},{10... | collective-permute-start | bytes 3145736 | tf_op jit(solution)/shard_map/ppermute | solution.py:64
  770.7 39.4 %collective-permute-start.145 = (bf16[1,688,128]{2,1,0:T(8,128)(2,1)}, bf16[1,688,128]{2,1,0:T(8,128)(2,1)S(1)}, u32[]{:S(2)}, u32[]{:S(2)}) collective-permute-start(bf16[1,688,128]{2,1,0:T(8,128)(2,1)} %bitcast.527), channel_id=1, source_target_pairs={{0,8},{8,0},{16,24},{24,16},{1,9},{9,1},{17,25},{25,17},{2,10},{10... | collective-permute-start | bytes 528392 | tf_op jit(solution)/shard_map/ppermute | solution.py:64
  771.7 40.5 %collective-permute-start.146 = (bf16[1,688,128]{2,1,0:T(8,128)(2,1)}, bf16[1,688,128]{2,1,0:T(8,128)(2,1)S(1)}, u32[]{:S(2)}, u32[]{:S(2)}) collective-permute-start(bf16[1,688,128]{2,1,0:T(8,128)(2,1)} %bitcast.526), channel_id=1, source_target_pairs={{0,16},{8,24},{16,0},{24,8},{1,17},{9,25},{17,1},{25,9},{2,18},{10... | collective-permute-start | bytes 528392 | tf_op jit(solution)/shard_map/ppermute | solution.py:64
  892.8 36.8 %collective-permute-start.148 = (bf16[4,1,688,64]{2,3,1,0:T(8,128)(2,1)}, bf16[4,1,688,64]{2,3,1,0:T(8,128)(2,1)}, u32[]{:S(2)}, u32[]{:S(2)}) collective-permute-start(bf16[4,1,688,64]{2,3,1,0:T(8,128)(2,1)} %get-tuple-element.126), channel_id=1, source_target_pairs={{0,1},{1,0},{2,3},{3,2},{4,5},{5,4},{6,7},{7,6},{8,9},{9,8},{10,11... | collective-permute-start | bytes 1056776 | tf_op jit(solution)/shard_map/ppermute | solution.py:58
  896.6 47.6 %collective-permute-start.141 = (bf16[4,2,688,64]{2,3,1,0:T(8,128)(2,1)}, bf16[4,2,688,64]{2,3,1,0:T(8,128)(2,1)}, u32[]{:S(2)}, u32[]{:S(2)}) collective-permute-start(bf16[4,2,688,64]{2,3,1,0:T(8,128)(2,1)} %get-tuple-element.80), channel_id=1, source_target_pairs={{0,1},{1,0},{2,3},{3,2},{4,5},{5,4},{6,7},{7,6},{8,9},{9,8},{10,11... | collective-permute-start | bytes 2113544 | tf_op jit(solution)/shard_map/ppermute | solution.py:58
  896.6 95.8 %collective-permute-start.116 = (bf16[4,4,64,2048]{3,2,0,1:T(8,128)(2,1)}, bf16[4,4,64,2048]{3,2,0,1:T(8,128)(2,1)}, u32[]{:S(2)}, u32[]{:S(2)}) collective-permute-start(bf16[4,4,64,2048]{3,2,0,1:T(8,128)(2,1)} %bitcast.519), channel_id=1, source_target_pairs={{0,1},{1,0},{2,3},{3,2},{4,5},{5,4},{6,7},{7,6},{8,9},{9,8},{10,11... | collective-permute-start | bytes 12582920 | tf_op jit(solution)/shard_map/ppermute | solution.py:58
  922.2 78.1 %collective-permute-start.108 = (bf16[4,4,64,2560]{3,2,0,1:T(8,128)(2,1)}, bf16[4,4,64,2560]{3,2,0,1:T(8,128)(2,1)}, u32[]{:S(2)}, u32[]{:S(2)}) collective-permute-start(bf16[4,4,64,2560]{3,2,0,1:T(8,128)(2,1)} %bitcast.518), channel_id=1, source_target_pairs={{0,1},{1,0},{2,3},{3,2},{4,5},{5,4},{6,7},{7,6},{8,9},{9,8},{10,11... | collective-permute-start | bytes 15728648 | tf_op jit(solution)/shard_map/ppermute | solution.py:58
  991.7 39.1 %collective-permute-start.131 = (f32[5,64]{1,0:T(8,128)S(1)}, f32[5,64]{1,0:T(8,128)S(1)}, u32[]{:S(2)}, u32[]{:S(2)}) collective-permute-start(f32[5,64]{1,0:T(8,128)S(1)} %bitcast_add_fusion.1), channel_id=1, source_target_pairs={{0,2},{1,3},{2,4},{3,5},{4,6},{5,7},{6,0},{7,1},{8,10},{9,11},{10,... | collective-permute-start | bytes 3848 | tf_op jit(solution)/shard_map/ppermute | solution.py:61
  1014.5 35.2 %collective-permute-start.120 = (bf16[4,64,2048]{2,1,0:T(8,128)(2,1)S(1)}, bf16[4,64,2048]{2,1,0:T(8,128)(2,1)S(1)}, u32[]{:S(2)}, u32[]{:S(2)}) collective-permute-start(bf16[4,64,2048]{2,1,0:T(8,128)(2,1)S(1)} %pad_maximum_fusion.11), channel_id=1, source_target_pairs={{0,16},{8,24},{16,0},{24,8},{1,17},{9,25},{17,1},{25,9},{2,18},{10... | collective-permute-start | bytes 3145736 | tf_op jit(solution)/shard_map/ppermute | solution.py:64
  1015.9 34.6 %collective-permute-start.118 = (bf16[4,64,2048]{2,1,0:T(8,128)(2,1)S(1)}, bf16[4,64,2048]{2,1,0:T(8,128)(2,1)S(1)}, u32[]{:S(2)}, u32[]{:S(2)}) collective-permute-start(bf16[4,64,2048]{2,1,0:T(8,128)(2,1)S(1)} %pad_maximum_fusion.10), channel_id=1, source_target_pairs={{0,8},{8,0},{16,24},{24,16},{1,9},{9,1},{17,25},{25,17},{2,10},{10... | collective-permute-start | bytes 3145736 | tf_op jit(solution)/shard_map/ppermute | solution.py:64
  1028.5 45.1 %collective-permute-start.112 = (bf16[4,64,2560]{2,1,0:T(8,128)(2,1)S(1)}, bf16[4,64,2560]{2,1,0:T(8,128)(2,1)S(1)}, u32[]{:S(2)}, u32[]{:S(2)}) collective-permute-start(bf16[4,64,2560]{2,1,0:T(8,128)(2,1)S(1)} %pad_maximum_fusion.4), channel_id=1, source_target_pairs={{0,16},{8,24},{16,0},{24,8},{1,17},{9,25},{17,1},{25,9},{2,18},{10... | collective-permute-start | bytes 3932168 | tf_op jit(solution)/shard_map/ppermute | solution.py:64
  1029.9 44.2 %collective-permute-start.110 = (bf16[4,64,2560]{2,1,0:T(8,128)(2,1)S(1)}, bf16[4,64,2560]{2,1,0:T(8,128)(2,1)S(1)}, u32[]{:S(2)}, u32[]{:S(2)}) collective-permute-start(bf16[4,64,2560]{2,1,0:T(8,128)(2,1)S(1)} %pad_maximum_fusion.3), channel_id=1, source_target_pairs={{0,8},{8,0},{16,24},{24,16},{1,9},{9,1},{17,25},{25,17},{2,10},{10... | collective-permute-start | bytes 3932168 | tf_op jit(solution)/shard_map/ppermute | solution.py:64
  (204 other events, 3765.0 us)
